TPU v7x, 32 devices: a whole 2x2x4 slice. The times are simulated.
32 devices in a mesh: rep: 4 (over y, x), exp: 8 (over z, core).
Axes of the slice: x: 2, y: 2, z: 4, core: 2. Of those that a mesh axis runs over, the one named last changes fastest.
Arguments:
- tokens: bfloat16 [4, 1024, 2048], P('rep', 'exp'), may hold values from -6 to 6
- cotangent: bfloat16 [4, 1024, 2048], P('rep', 'exp'), may hold values from -12 to 12
- route_weight: float32 [4, 1024, 8], P('rep', 'exp'), may hold values from 0.05 to 0.25
- expert_ids: int32 [4, 1024, 8], P('rep', 'exp'), may hold values from 0 to 15, as said below
- slots: int32 [4, 1024, 8], P('rep', 'exp'), may hold values from 0 to 127, as said below
- gossip_round: int32 [1], replicated, may hold values from 0 to 127
- w_in: bfloat16 [4, 16, 2048, 768], P('rep', 'exp'), may hold values from -4 to 4
- w_out: bfloat16 [4, 16, 384, 2048], P('rep', 'exp'), may hold values from -4 to 4
- mom_in: bfloat16 [4, 16, 2048, 768], P('rep', 'exp'), may hold values from -3 to 3
- mom_out: bfloat16 [4, 16, 384, 2048], P('rep', 'exp'), may hold values from -3 to 3
Outputs:
- layer_out: bfloat16 [4, 1024, 2048], P('rep', 'exp')
- grad_tokens: bfloat16 [4, 1024, 2048], P('rep', 'exp')
- new_w_in: bfloat16 [4, 16, 2048, 768], P('rep', 'exp')
- new_w_out: bfloat16 [4, 16, 384, 2048], P('rep', 'exp')
- new_mom_in: bfloat16 [4, 16, 2048, 768], P('rep', 'exp')
- new_mom_out: bfloat16 [4, 16, 384, 2048], P('rep', 'exp')
Inputs may be any that keep to these rules, and one draw needn't show every extreme that they name: `expert_ids`: each token names 8 different experts. `slots`: the slot of a choice is the number of earlier tokens of the same aligned block of 128 tokens of its replica that name the same expert; in every block some expert is named by all tokens. `gossip_round`: the peer of replica k is k xor 2^(t mod 2).
All inputs are finite; a program needn't handle non-finite values.
Results may differ from a plain program's by a relative error of at most 0.0052.
Values may be sent and summed in bfloat16 or wider, within the bound.
No kernel may reach another device: no remote copies, remote signals or barrier semaphores. Data moves between devices by JAX's collectives and lax.ppermute only.
A program may use at most 128 MiB of HBM per device.

v0:
```python
from functools import partial
import math

import jax
import jax.numpy as jnp
from jax import lax
from jax.experimental import pallas as pl
from jax.experimental.pallas import tpu as pltpu
from jax.sharding import PartitionSpec as P

CAP = 64
MOMENTUM_DECAY = 0.9
STEP_SIZE = 0.2
COLS = 512
DEEP = 256
SCALARS = ()
PIECES = (4, 4, 9, 7)
F32 = jnp.float32
BF16 = jnp.bfloat16
VMEM = 32 * 1024 * 1024


def to_xor(value, k):
    size = lax.axis_size("exp")
    return lax.ppermute(value, "exp", [(i, i ^ k) for i in range(size)])


def swap(value):
    return to_xor(value, 1)


def along_chips(value, targets):
    return lax.ppermute(value, "exp", [(2 * c + k, 2 * t + k) for c, t in enumerate(targets) for k in range(2)])


def gossip(value, bit):
    size = lax.axis_size("rep")
    return lax.ppermute(value, "rep", [(i, i ^ (1 << bit)) for i in range(size)])


def after(value, *first):
    return lax.optimization_barrier((value, *first))[0]


def near_and_far(value):
    chips = lax.axis_size("exp") // 2
    if chips != 4:
        return [to_xor(value, 2 * s) for s in range(1, chips)]
    far = to_xor(value, 6)
    return [to_xor(value, 2), far]


def all_blocks(value, found, relayed):
    if len(found) != 2:
        return [value] + list(found)
    return [value, found[0], along_chips(relayed, (2, 0, 3, 1)), found[1]]


def with_other_core(same):
    return [part for block in same for part in (block, swap(block))]


def send_first(parts, *first):
    parts = lax.optimization_barrier((*parts, *first))[: len(parts)]
    if len(parts) != 3:
        return [to_xor(part, 2 * s + 2) for s, part in enumerate(parts)]
    return [along_chips(parts[1], (1, 3, 0, 2)), to_xor(parts[0], 2)]


def nn(a, b):
    return jnp.dot(a, b, preferred_element_type=F32)


def nt(a, b):
    return lax.dot_general(a, b, (((1,), (1,)), ((), ())), preferred_element_type=F32)


def tn(a, b):
    return lax.dot_general(a, b, (((0,), (0,)), ((), ())), preferred_element_type=F32)


def kernel_call(body, grid, ins, outs, scratch=(), flops=0, aliases=None, kept=()):
    in_hbm = pltpu.HBM

    def spec(block, where):
        if block is None:
            return pl.BlockSpec(memory_space=pl.ANY)
        if block is SCALARS:
            return pl.BlockSpec(memory_space=pltpu.SMEM)
        return pl.BlockSpec(block, where)

    moved = sum(math.prod(a.shape) * a.dtype.itemsize for a, block, _ in list(ins) + list(outs) if block is not None)
    return pl.pallas_call(
        body,
        grid=grid,
        in_specs=[spec(b, w) for _, b, w in ins],
        out_specs=[spec(b, w) for _, b, w in outs],
        out_shape=[in_hbm(a.shape, a.dtype) if k in kept else jax.ShapeDtypeStruct(a.shape, a.dtype) for k, (a, _, _) in enumerate(outs)],
        scratch_shapes=list(scratch),
        input_output_aliases=aliases or {},
        compiler_params=pltpu.CompilerParams(vmem_limit_bytes=VMEM),
        cost_estimate=pl.CostEstimate(flops=flops // 3, bytes_accessed=moved // 3, transcendentals=0),
    )(*[a for a, _, _ in ins])


def shape(dims, dtype):
    return jax.ShapeDtypeStruct(dims, dtype)


def matches(mine_ref, k, local):
    tokens = mine_ref.shape[2]
    slot = lax.broadcasted_iota(jnp.int32, (CAP, tokens), 0).astype(F32)
    return [mine_ref[k, 2 * a : 2 * a + 1, :] == slot for a in range(local)]


def onehot(found):
    return jnp.concatenate([f.astype(F32) for f in found], axis=0).astype(BF16)


def row_weights(mine_ref, k, found):
    return [
        jnp.sum(jnp.where(f, mine_ref[k, 2 * a + 1 : 2 * a + 2, :], 0.0), axis=1, keepdims=True)
        for a, f in enumerate(found)
    ]


def fill_rows(blocks, mine_ref, rows_ref, local, weighted):
    for k, block in enumerate(blocks):
        found = matches(mine_ref, k, local)
        rows = nn(onehot(found), block[...])
        weight = row_weights(mine_ref, k, found) if weighted else None
        for a in range(local):
            part = rows[a * CAP : (a + 1) * CAP]
            if weighted:
                part = part * weight[a]
            rows_ref[a, k * CAP : (k + 1) * CAP, :] = part.astype(BF16)


def forward_body(groups, local, hidden, scale, *refs):
    blocks, (mine, w, rows, inner, slope, value, joint) = refs[:groups], refs[groups:]
    fill_rows(blocks, mine, rows, local, False)
    first = pl.program_id(0) == 0

    for a in range(local):
        part = nn(rows[a], w[a])

        @pl.when(first)
        def _():
            joint[a] = part

        @pl.when(jnp.logical_not(first))
        def _():
            joint[a] += part

    @pl.when(pl.program_id(0) == pl.num_programs(0) - 1)
    def _():
        for a in range(local):
            gate = joint[a, :, :hidden] * scale
            upper = joint[a, :, hidden:] * scale
            sigmoid = jax.nn.sigmoid(gate)
            act = gate * sigmoid
            inner[a] = (act * upper).astype(BF16)
            slope[a] = upper * (sigmoid * (1.0 + gate * (1.0 - sigmoid)))
            value[a] = act


def forward(blocks, mine, proj_in):
    groups = len(blocks)
    local, width, double = proj_in.shape
    hidden, rows, tokens = double // 2, groups * CAP, blocks[0].shape[0]
    whole = lambda j: (0, 0, 0)
    return kernel_call(
        partial(forward_body, groups, local, hidden, 1.0 / math.sqrt(width)),
        (width // COLS,),
        [(b, (tokens, COLS), lambda j: (0, j)) for b in blocks]
        + [(mine, mine.shape, whole), (proj_in, (local, COLS, double), lambda j: (0, j, 0))],
        [
            (shape((local, rows, width), BF16), (local, rows, COLS), lambda j: (0, 0, j)),
            (shape((local, rows, hidden), BF16), (local, rows, hidden), whole),
            (shape((local, rows, hidden), F32), (local, rows, hidden), whole),
            (shape((local, rows, hidden), F32), (local, rows, hidden), whole),
        ],
        [pltpu.VMEM((local, rows, double), F32)],
        2 * local * rows * width * double,
    )


def backward_body(groups, local, hidden, scale, *refs):
    blocks = refs[:groups]
    mine, inner, slope, value, w, mom, new_mom, update, grad_joint, rows, grad_inner = refs[groups:]
    fill_rows(blocks, mine, rows, local, True)
    first = pl.program_id(0) == 0

    for a in range(local):
        moment = MOMENTUM_DECAY * mom[a].astype(F32) + tn(inner[a], rows[a]) * scale
        new_mom[a] = moment.astype(BF16)
        update[a] = (w[a].astype(F32) - STEP_SIZE * moment).astype(BF16)
        part = nt(rows[a], w[a])

        @pl.when(first)
        def _():
            grad_inner[a] = part

        @pl.when(jnp.logical_not(first))
        def _():
            grad_inner[a] += part

    @pl.when(pl.program_id(0) == pl.num_programs(0) - 1)
    def _():
        for a in range(local):
            grad = grad_inner[a] * scale
            grad_joint[a, :, :hidden] = (grad * slope[a]).astype(BF16)
            grad_joint[a, :, hidden:] = (grad * value[a]).astype(BF16)


def backward(blocks, mine, inner, slope, value, proj_out, mom_out):
    groups = len(blocks)
    local, hidden, width = proj_out.shape
    rows, tokens = groups * CAP, blocks[0].shape[0]
    whole = lambda j: (0, 0, 0)
    cut = ((local, hidden, COLS), lambda j: (0, 0, j))
    held = ((local, rows, hidden), whole)
    return kernel_call(
        partial(backward_body, groups, local, hidden, 1.0 / math.sqrt(hidden)),
        (width // COLS,),
        [(b, (tokens, COLS), lambda j: (0, j)) for b in blocks]
        + [(mine, mine.shape, whole), (inner, *held), (slope, *held), (value, *held), (proj_out, *cut), (mom_out, *cut)],
        [
            (proj_out, *cut),
            (proj_out, *cut),
            (shape((local, rows, 2 * hidden), BF16), (local, rows, 2 * hidden), whole),
        ],
        [pltpu.VMEM((local, rows, COLS), BF16), pltpu.VMEM((local, rows, hidden), F32)],
        4 * local * rows * width * hidden,
        kept=(0,),
    )


def peer_body(groups, local, scale, *refs):
    blocks, (mine, inner, *bases, update, new_w, rows) = refs[:groups], refs[groups:]
    fill_rows(blocks, mine, rows, local, True)
    for a in range(local):
        whole = jnp.concatenate([base[a].astype(F32) for base in bases], axis=0)
        theirs = whole - STEP_SIZE * (tn(inner[a], rows[a]) * scale)
        new_w[a] = (0.5 * (update[a].astype(F32) + theirs)).astype(BF16)


def peer_out(blocks, mine, inner, bases, update):
    groups = len(blocks)
    local, hidden, width = update.shape
    rows, tokens = groups * CAP, blocks[0].shape[0]
    whole = lambda j: (0, 0, 0)
    cut = ((local, hidden, COLS), lambda j: (0, 0, j))
    return kernel_call(
        partial(peer_body, groups, local, 1.0 / math.sqrt(hidden)),
        (width // COLS,),
        [(b, (tokens, COLS), lambda j: (0, j)) for b in blocks]
        + [(mine, mine.shape, whole), (inner, (local, rows, hidden), whole)]
        + [(b, (local, b.shape[1], COLS), lambda j: (0, 0, j)) for b in bases]
        + [(update, *cut)],
        [(update, *cut)],
        [pltpu.VMEM((local, rows, COLS), BF16)],
        2 * local * rows * width * hidden,
        kept=(0,),
    )[0]


def base_body(w, mom, *bases):
    whole = (w[...].astype(F32) - (STEP_SIZE * MOMENTUM_DECAY) * mom[...].astype(F32)).astype(BF16)
    start = 0
    for base in bases:
        base[...] = whole[:, start : start + base.shape[1]]
        start += base.shape[1]


def base_out(proj_out, mom_out):
    local, hidden, width = proj_out.shape
    cut = ((local, hidden, COLS), lambda j: (0, 0, j))
    unit = hidden // 24
    outs = [(shape((local, n * unit, width), BF16), (local, n * unit, COLS), lambda j: (0, 0, j)) for n in PIECES]
    kept = range(len(outs))
    return kernel_call(base_body, (width // COLS,), [(proj_out, *cut), (mom_out, *cut)], outs, kept=kept)


def grad_in_body(scale, rows, grad_joint, w, mom, *rest):
    update, new_mom = rest[-2:]
    moment = MOMENTUM_DECAY * mom[0].astype(F32) + tn(rows[0], grad_joint[0]) * scale
    new_mom[0] = moment.astype(BF16)
    update[0] = (w[0].astype(F32) - STEP_SIZE * moment).astype(BF16)


def grad_in(rows_in, grad_joint, proj_in, mom_in, start, depth, held):
    local, width, double = proj_in.shape
    rows = rows_in.shape[1]
    first = start // DEEP
    cut = ((1, DEEP, double), lambda a, i: (a, first + i, 0))
    ins = [
        (rows_in, (1, rows, DEEP), lambda a, i: (a, 0, first + i)),
        (grad_joint, (1, rows, double), lambda a, i: (a, 0, 0)),
        (proj_in, *cut),
        (mom_in, *cut),
    ]
    if held is not None:
        ins.append((held, None, None))
    return kernel_call(
        partial(grad_in_body, 1.0 / math.sqrt(width)),
        (local, depth // DEEP),
        ins,
        [(shape((local, depth, double), BF16), (1, DEEP, double), lambda a, i: (a, i, 0)), (proj_in, *cut)],
        flops=2 * local * rows * depth * double,
        aliases={4: 1} if held is not None else None,
        kept=(1,),
    )


def average_body(own, peer, *rest):
    rest[-1][...] = (0.5 * (own[...].astype(F32) + peer[...].astype(F32))).astype(BF16)


def average(own, peer, like, start, held):
    local, depth, double = own.shape
    block = (1, DEEP, double)
    ins = [(own, block, lambda a, i: (a, i, 0)), (peer, block, lambda a, i: (a, i, 0))]
    if held is not None:
        ins.append((held, None, None))
    return kernel_call(
        average_body,
        (local, depth // DEEP),
        ins,
        [(like, block, lambda a, i: (a, start // DEEP + i, 0))],
        aliases={2: 0} if held is not None else None,
        kept=(0,),
    )[0]


def returns_body(groups, local, scale, weighted, product, left, w, mine, own, other, rows):
    for a in range(local):
        rows[a] = (product(left[a], w[a]) * scale).astype(rows.dtype)
    for k in range(groups):
        found = matches(mine, k, local)
        weight = row_weights(mine, k, found) if weighted else None
        parts = [rows[a, k * CAP : (k + 1) * CAP, :] for a in range(local)]
        if weighted:
            parts = [p * weight[a] for a, p in enumerate(parts)]
        part = tn(onehot(found), jnp.concatenate([p.astype(BF16) for p in parts], axis=0))
        if k % 2 == 0:
            own[k // 2] = part
        else:
            other[k // 2] = part.astype(BF16)


def returns(left, w, mine, weighted):
    groups, _, tokens = mine.shape
    local, rows, inside = left.shape
    whole = lambda j: (0, 0, 0)
    if weighted:
        product, width, cut, scale = nn, w.shape[2], ((local, inside, COLS), lambda j: (0, 0, j)), 1.0 / math.sqrt(inside)
    else:
        product, width, cut, scale = nt, w.shape[1], ((local, COLS, inside), lambda j: (0, j, 0)), 1.0 / math.sqrt(w.shape[1])
    out = ((groups // 2, tokens, COLS), lambda j: (0, 0, j))
    return kernel_call(
        partial(returns_body, groups, local, scale, weighted, product),
        (width // COLS,),
        [(left, left.shape, whole), (w, *cut), (mine, mine.shape, whole)],
        [(shape((groups // 2, tokens, width), F32), *out), (shape((groups // 2, tokens, width), BF16), *out)],
        [pltpu.VMEM((local, rows, COLS), F32 if weighted else BF16)],
        2 * local * rows * width * inside,
    )


def columns(array):
    lead = array.shape[:-1]
    return array, (*lead, COLS) if lead else SCALARS, lambda j: (*(0 for _ in lead), j)


def line_end():
    chip = lax.axis_index("exp") // 2
    return ((chip == 0) | (chip == 3)).astype(jnp.int32)[None]


def by_columns(body, ins, outs, kept=()):
    return kernel_call(body, (outs[0].shape[-1] // COLS,), [columns(a) for a in ins], [columns(a) for a in outs], kept=kept)


def middle_body(ends, value, far, out):
    out[...] = jnp.where(ends[0] > 0, value[...], far[...])


def middle_of(value, found, ends):
    if len(found) != 2:
        return value
    return by_columns(middle_body, [ends, value, found[1]], [value])[0]


def paired_body(base, own, other, total, *parts):
    total[...] = base[...].astype(F32) + (own[0] + other[0].astype(F32))
    for s, part in enumerate(parts):
        part[...] = (own[s + 1] + other[s + 1].astype(F32)).astype(BF16)


def paired(base, own, other):
    out = by_columns(paired_body, [base, own, swap(other)], [shape(base.shape, F32)] + [base] * (own.shape[0] - 1))
    return out[0], out[1:]


def far_body(ends, part, middle, out):
    heard = jnp.where(ends[0] > 0, 0.0, middle[...].astype(F32))
    out[...] = (part[...].astype(F32) + heard).astype(BF16)


def send_last(parts, heard, ends):
    if len(parts) != 3:
        return heard
    far = by_columns(far_body, [ends, parts[2], heard[0]], [parts[2]])[0]
    return [*heard, to_xor(far, 6)]


def added_body(line, ends, total, *refs):
    out, heard = refs[-1], [ref[...].astype(F32) for ref in refs[:-1]]
    if line:
        heard[0] = jnp.where(ends[0] > 0, heard[0], 0.0)
    out[...] = sum(heard, total[...]).astype(BF16)


def added(total, heard, ends):
    line = lax.axis_size("exp") == 8
    return by_columns(partial(added_body, line), [ends, total, *heard], [shape(total.shape, BF16)], (0,))[0]


def routing(weights, chosen, places, local):
    groups = lax.axis_size("exp")
    tokens = chosen.shape[0]
    ids = jnp.arange(groups * local, dtype=jnp.int32)[:, None, None]
    hit = (chosen[None] == ids) & (places[None] < CAP)
    place_of = (jnp.sum(jnp.where(hit, places[None] + 1, 0), axis=2) - 1).astype(F32)
    weight_of = jnp.sum(jnp.where(hit, weights[None], 0.0), axis=2)
    packed = jnp.stack([place_of, weight_of], axis=1).reshape(groups, 2 * local, tokens)
    arrived = lax.all_to_all(packed, "exp", split_axis=0, concat_axis=0, tiled=True)
    return arrived[lax.axis_index("exp") ^ jnp.arange(groups, dtype=jnp.int32)]


def step(inputs, upstream, weights, chosen, places, proj_in, proj_out, mom_in, mom_out, bit):
    local, width, _ = proj_in.shape
    depth = 512

    ties = lax.optimization_barrier
    ends = line_end()
    first_rows = 3 * DEEP

    tok = near_and_far(inputs)
    peer_upstream = gossip(upstream, bit)
    mine = routing(weights, chosen, places, local)
    bases = base_out(proj_out, mom_out)
    peer_bases = [gossip(after(bases[0], peer_upstream), bit)]
    *tok, mine, peer_upstream, peer_bases[0] = ties((*tok, mine, peer_upstream, peer_bases[0]))
    sent = middle_of(inputs, tok, ends)
    tok_same = all_blocks(inputs, tok, sent)
    peer_bases.append(gossip(after(bases[1], sent), bit))
    peer_mine = gossip(after(mine, sent), bit)

    *tok_same, peer_bases[1], peer_mine = ties((*tok_same, peer_bases[1], peer_mine))
    upstream_now, base = ties((upstream, bases[2], *tok_same[1:], peer_bases[1]))[:2]
    cot = near_and_far(upstream_now)
    peer_bases.append(gossip(base, bit))
    rows_in, inner, slope, value = forward(with_other_core(tok_same), mine, proj_in)
    own, other = returns(inner, proj_out, mine, True)
    *cot, own, peer_bases[2] = ties((*cot, own, peer_bases[2]))
    sent = middle_of(upstream, cot, ends)
    cot_same = all_blocks(upstream, cot, sent)
    peer_inner = gossip(after(inner, sent), bit)
    total_1, parts_1 = paired(inputs, own, after(other, sent))

    *cot_same, total_1, peer_inner = ties((*cot_same, total_1, peer_inner))
    peer_bases.append(gossip(after(bases[3], peer_inner), bit))
    cot_all = with_other_core(cot_same)
    new_mom_out, update_out, grad_joint = backward(cot_all, mine, inner, slope, value, proj_out, mom_out)
    update_0, new_mom_in = grad_in(rows_in, grad_joint, proj_in, mom_in, 0, first_rows, None)
    peer_0 = gossip(update_0, bit)
    peer_upstream, new_mom_in, peer_bases[3] = ties((peer_upstream, new_mom_in, peer_bases[3]))
    heard_1 = send_first(parts_1, new_mom_in)
    there = near_and_far(peer_upstream)
    last = width - DEEP
    update_1, new_mom_in = grad_in(rows_in, grad_joint, proj_in, mom_in, first_rows, last - first_rows, new_mom_in)
    peer_1 = gossip(update_1, bit)
    update_2, new_mom_in = grad_in(rows_in, grad_joint, proj_in, mom_in, last, DEEP, new_mom_in)
    peer_2 = gossip(update_2, bit)
    own, other = returns(after(grad_joint, update_2), proj_in, mine, False)

    *there, own, heard_1[0] = ties((*there, own, *heard_1))[: len(there) + 2]
    heard_1 = send_last(parts_1, heard_1, ends)
    sent = middle_of(peer_upstream, there, ends)
    there_same = all_blocks(peer_upstream, there, sent)
    total_2, parts_2 = paired(upstream, own, after(other, sent))
    new_w_in = average(update_0, after(peer_0, total_2), proj_in, 0, None)

    *there_same, new_w_in, heard_1[-1] = ties((*there_same, new_w_in, heard_1[-1]))
    layer_out = added(total_1, heard_1, ends)
    heard_2 = send_first(parts_2, there_same[2])
    there_all = with_other_core(there_same)
    new_w_out = peer_out(there_all, peer_mine, peer_inner, peer_bases, update_out)
    *heard_2, new_w_out, layer_out = ties((*heard_2, new_w_out, layer_out))
    grad_tokens = added(total_2, send_last(parts_2, heard_2, ends), ends)

    new_w_in = average(update_1, after(peer_1, grad_tokens), proj_in, first_rows, new_w_in)
    new_w_in = average(update_2, peer_2, proj_in, last, new_w_in)
    return tuple(v[None] for v in (layer_out, grad_tokens, new_w_in, new_w_out, new_mom_in, new_mom_out))


def shards(tokens, cotangent, route_weight, expert_ids, slots, gossip_round, w_in, w_out, mom_in, mom_out):
    levels = lax.axis_size("rep").bit_length() - 1
    round_now = jnp.remainder(gossip_round[0], jnp.int32(levels))
    operands = [v[0] for v in (tokens, cotangent, route_weight, expert_ids, slots, w_in, w_out, mom_in, mom_out)]
    return lax.switch(round_now, [partial(step, bit=bit) for bit in range(levels)], *operands)


def solution(mesh):
    three, four = P("rep", "exp", None), P("rep", "exp", None, None)
    return jax.shard_map(
        shards,
        mesh=mesh,
        in_specs=(three, three, three, three, three, P(), four, four, four, four),
        out_specs=(three, three, four, four, four, four),
        check_vma=False,
    )
```

profile of v0, /device:TPU:0, one launch (start us, length us, event | category | flops | bytes accessed | tf_op | source)
XLA Modules:
  0.0 264.6 jit_solution(17307684667778156767)
XLA Ops:
  1.3 263.2 %conditional.1 = (bf16[1,128,2048]{2,1,0:T(8,128)(2,1)}, bf16[1,128,2048]{2,1,0:T(8,128)(2,1)}, bf16[1,2,2048,768]{3,2,1,0:T(8,128)(2,1)}, bf16[1,2,384,2048]{3,...) conditional(s32[]{:T(128)} %clamp.3, (bf16[128,2048]{1,0:T(8,128)(2,1)}, ...), branch_computations={%region_0.3_spmd, %region_3.6_spmd} | conditional | flops 5368847360 | bytes 258135552 | solution.py:513
  9.1 5.0 %branch_0_fun.21 = (bf16[2,64,2048]{2,1,0:T(8,128)(2,1)}, bf16[2,64,2048]{2,1,0:T(8,128)(2,1)}, bf16[2,144,2048]{2,1,0:T(8,128)(2,1)}, bf16[2,112,2048]{2,1,0:T(8,128)(2,1)}) custom-call(bf16[2,384,2048]{2,1,0:T(8,128)(2,1)} %get-tuple-element.41.w.refs_12_, bf16[2,384,2048]{2,1,0:T(8,128)(2,1)} %get-tuple-element.42.mom.refs_13_), custom_call_target="tpu_custom_call" | custom-call | bytes 3145728 | tf_op jit(solution)/shard_map/cond/branch_0_fun/pallas_call | solution.py:93
  14.2 6.0 %collective-permute-done.2.value.refs_0_ = bf16[128,2048]{1,0:T(8,128)(2,1)S(1)} collective-permute-done((bf16[128,2048]{1,0:T(8,128)(2,1)}, bf16[128,2048]{1,0:T(8,128)(2,1)S(1)}, u32[]{:S(2)}, u32[]{:S(2)}) %collective-permute-start.2) | collective-permute-done | bytes 524320 | tf_op jit(solution)/shard_map/cond/branch_0_fun/ppermute | solution.py:38
  25.7 5.5 %all-to-all-done = f32[8,4,128]{2,1,0:T(4,128)S(1)} async-done(((f32[8,4,128]{2,1,0:T(4,128)}), f32[8,4,128]{2,1,0:T(4,128)S(1)}, u32[]{:S(2)}, u32[]{:S(2)}) %all-to-all-start) | async-done | bytes 16416 | tf_op jit(solution)/shard_map/cond/branch_0_fun/all_to_all | solution.py:438
  35.6 10.7 %collective-permute-done.6.refs_8_ = f32[8,4,128]{2,1,0:T(4,128)S(1)} collective-permute-done((f32[8,4,128]{2,1,0:T(4,128)S(1)}, f32[8,4,128]{2,1,0:T(4,128)S(1)}, u32[]{:S(2)}, u32[]{:S(2)}) %collective-permute-start.6) | collective-permute-done | bytes 16416 | tf_op jit(solution)/shard_map/cond/branch_0_fun/ppermute | solution.py:38
  53.3 10.9 %branch_0_fun.23 = (bf16[2,512,2048]{2,1,0:T(8,128)(2,1)S(1)}, bf16[2,512,384]{2,1,0:T(8,128)(2,1)S(1)}, f32[2,512,384]{2,1,0:T(8,128)S(1)}, f32[2,512,384]{2,1,0:T(8,128)S(1)}) custom-call(bf16[128,2048]{1,0:T(8,128)(2,1)S(1)} %copy-done.34, bf16[128,2048]{1,0:T(8,128)(2,1)S(1)} %collective-permute-done.7.refs_1_, ...), custom_call_target="tpu_custom_call" | custom-call | flops 1073741824 | bytes 6209536 | tf_op jit(solution)/shard_map/cond/branch_0_fun/pallas_call | solution.py:93
  64.2 4.6 %branch_0_fun.24 = (f32[4,128,2048]{2,1,0:T(8,128)S(1)}, bf16[4,128,2048]{2,1,0:T(8,128)(2,1)S(1)}) custom-call(bf16[2,512,384]{2,1,0:T(8,128)(2,1)S(1)} %get-tuple-element.70.left.refs_9_, bf16[2,384,2048]{2,1,0:T(8,128)(2,1)S(1)} %copy-done.32, f32[8,4,128]{2,1,0:T(4,128)S(1)} %gather_fusion), custom_call_target="tpu_custom_call" | custom-call | flops 536870912 | bytes 3413333 | tf_op jit(solution)/shard_map/cond/branch_0_fun/pallas_call | solution.py:93
  68.9 7.9 %collective-permute-done.12.far.refs_6_ = bf16[128,2048]{1,0:T(8,128)(2,1)S(1)} collective-permute-done((bf16[128,2048]{1,0:T(8,128)(2,1)}, bf16[128,2048]{1,0:T(8,128)(2,1)S(1)}, u32[]{:S(2)}, u32[]{:S(2)}) %collective-permute-start.12) | collective-permute-done | bytes 524320 | tf_op jit(solution)/shard_map/cond/branch_0_fun/ppermute | solution.py:25
  82.4 10.0 %collective-permute-done.14.refs_4_ = bf16[128,2048]{1,0:T(8,128)(2,1)S(1)} collective-permute-done((bf16[128,2048]{1,0:T(8,128)(2,1)S(1)}, bf16[128,2048]{1,0:T(8,128)(2,1)S(1)}, u32[]{:S(2)}, u32[]{:S(2)}) %collective-permute-start.14) | collective-permute-done | bytes 524320 | tf_op jit(solution)/shard_map/cond/branch_0_fun/ppermute | solution.py:33
  92.3 4.7 %collective-permute-done.16.refs_9_ = bf16[2,512,384]{2,1,0:T(8,128)(2,1)S(1)} collective-permute-done((bf16[2,512,384]{2,1,0:T(8,128)(2,1)S(1)}, bf16[2,512,384]{2,1,0:T(8,128)(2,1)S(1)}, u32[]{:S(2)}, u32[]{:S(2)}) %collective-permute-start.16) | collective-permute-done | bytes 786464 | tf_op jit(solution)/shard_map/cond/branch_0_fun/ppermute | solution.py:38
  103.3 10.6 %branch_0_fun.27 = (bf16[2,384,2048]{2,1,0:T(8,128)(2,1)}, bf16[2,384,2048]{2,1,0:T(8,128)(2,1)S(1)}, bf16[2,512,768]{2,1,0:T(8,128)(2,1)S(1)}) custom-call(bf16[128,2048]{1,0:T(8,128)(2,1)S(1)} %copy-done.38, bf16[128,2048]{1,0:T(8,128)(2,1)S(1)} %collective-permute-done.17.refs_1_, bf16[128,2048]{1,0:T(8,128)(2,1)S(1)} %collective-permute-done.11.refs_2_, ...), custom_call_target="tpu_custom_call" | custom-call | flops 1073741824 | bytes 7432874 | tf_op jit(solution)/shard_map/cond/branch_0_fun/pallas_call | solution.py:93
  113.8 6.5 %branch_0_fun.28 = (bf16[2,768,768]{2,1,0:T(8,128)(2,1)S(1)}, bf16[2,2048,768]{2,1,0:T(8,128)(2,1)}) custom-call(bf16[2,512,2048]{2,1,0:T(8,128)(2,1)S(1)} %get-tuple-element.57.rows, bf16[2,512,768]{2,1,0:T(8,128)(2,1)S(1)} %get-tuple-element.87.grad_joint.left, bf16[2,2048,768]{2,1,0:T(8,128)(2,1)} %get-tuple-element.56.refs_9_.w, ...), custom_call_target="tpu_custom_call" | custom-call | flops 402653184 | bytes 9000277 | tf_op jit(solution)/shard_map/cond/branch_0_fun/pallas_call | solution.py:93
  127.0 8.3 %branch_0_fun.29 = (bf16[2,1024,768]{2,1,0:T(8,128)(2,1)S(1)}, bf16[2,2048,768]{2,1,0:T(8,128)(2,1)}) custom-call(bf16[2,512,2048]{2,1,0:T(8,128)(2,1)S(1)} %get-tuple-element.57.rows, bf16[2,512,768]{2,1,0:T(8,128)(2,1)S(1)} %get-tuple-element.87.grad_joint.left, ...), custom_call_target="tpu_custom_call", output_to_operand_aliasing={{1}: (4, {})} | custom-call | flops 536870912 | bytes 9262421 | tf_op jit(solution)/shard_map/cond/branch_0_fun/pallas_call | solution.py:93
  138.3 7.0 %branch_0_fun.31 = (f32[4,128,2048]{2,1,0:T(8,128)S(1)}, bf16[4,128,2048]{2,1,0:T(8,128)(2,1)S(1)}) custom-call(bf16[2,512,768]{2,1,0:T(8,128)(2,1)S(1)} %get-tuple-element.87.grad_joint.left, bf16[2,2048,768]{2,1,0:T(8,128)(2,1)} %get-tuple-element.56.refs_9_.w, f32[8,4,128]{2,1,0:T(4,128)S(1)} %gather_fusion), custom_call_target="tpu_custom_call" | custom-call | flops 1073741824 | bytes 4724053 | tf_op jit(solution)/shard_map/cond/branch_0_fun/pallas_call | solution.py:93
  147.3 10.5 %collective-permute-done.22.refs_2_ = bf16[128,2048]{1,0:T(8,128)(2,1)S(1)} collective-permute-done((bf16[128,2048]{1,0:T(8,128)(2,1)S(1)}, bf16[128,2048]{1,0:T(8,128)(2,1)S(1)}, u32[]{:S(2)}, u32[]{:S(2)}) %collective-permute-start.22) | collective-permute-done | bytes 524320 | tf_op jit(solution)/shard_map/cond/branch_0_fun/ppermute | solution.py:25
  157.8 11.9 %collective-permute-done.23.far.refs_6_ = bf16[128,2048]{1,0:T(8,128)(2,1)S(1)} collective-permute-done((bf16[128,2048]{1,0:T(8,128)(2,1)S(1)}, bf16[128,2048]{1,0:T(8,128)(2,1)S(1)}, u32[]{:S(2)}, u32[]{:S(2)}) %collective-permute-start.23) | collective-permute-done | bytes 524320 | tf_op jit(solution)/shard_map/cond/branch_0_fun/ppermute | solution.py:25
  183.1 5.1 %collective-permute-done.29.refs_2_ = bf16[128,2048]{1,0:T(8,128)(2,1)S(1)} collective-permute-done((bf16[128,2048]{1,0:T(8,128)(2,1)S(1)}, bf16[128,2048]{1,0:T(8,128)(2,1)S(1)}, u32[]{:S(2)}, u32[]{:S(2)}) %collective-permute-start.29) | collective-permute-done | bytes 524320 | tf_op jit(solution)/shard_map/cond/branch_0_fun/ppermute | solution.py:25
  188.2 9.9 %collective-permute-done.27.refs_4_ = bf16[128,2048]{1,0:T(8,128)(2,1)S(1)} collective-permute-done((bf16[128,2048]{1,0:T(8,128)(2,1)S(1)}, bf16[128,2048]{1,0:T(8,128)(2,1)S(1)}, u32[]{:S(2)}, u32[]{:S(2)}) %collective-permute-start.27) | collective-permute-done | bytes 524320 | tf_op jit(solution)/shard_map/cond/branch_0_fun/ppermute | solution.py:33
  200.0 8.5 %collective-permute-start.30 = (bf16[128,2048]{1,0:T(8,128)(2,1)S(1)}, bf16[128,2048]{1,0:T(8,128)(2,1)S(1)}, u32[]{:S(2)}, u32[]{:S(2)}) collective-permute-start(bf16[128,2048]{1,0:T(8,128)(2,1)S(1)} %copy-done.29), channel_id=1, source_target_pairs={{0,2},{1,3},{2,6},{3,7},{4,0},{5,1},{6,4},{7,5},{8,10},{9,11},{10,... | collective-permute-start | bytes 1572872 | tf_op jit(solution)/shard_map/cond/branch_0_fun/ppermute | solution.py:33
  212.3 5.7 %branch_0_fun.36 = bf16[2,384,2048]{2,1,0:T(8,128)(2,1)} custom-call(bf16[128,2048]{1,0:T(8,128)(2,1)S(1)} %collective-permute-done.2.value.refs_0_, bf16[128,2048]{1,0:T(8,128)(2,1)S(1)} %collective-permute-done.32.refs_1_, bf16[128,2048]{1,0:T(8,128)(2,1)S(1)} %copy-done.17, bf16[128,2048]{1,0:T(8,128)(2,1)S(1)} %collective-permute-done.33.refs_3_, ...), custom_call_target="tpu_custom_call" | custom-call | flops 536870912 | bytes 4811434 | tf_op jit(solution)/shard_map/cond/branch_0_fun/pallas_call | solution.py:93
  218.0 4.0 %collective-permute-done.30.middle.refs_0_ = bf16[128,2048]{1,0:T(8,128)(2,1)S(1)} collective-permute-done((bf16[128,2048]{1,0:T(8,128)(2,1)S(1)}, bf16[128,2048]{1,0:T(8,128)(2,1)S(1)}, u32[]{:S(2)}, u32[]{:S(2)}) %collective-permute-start.30) | collective-permute-done | bytes 524320 | tf_op jit(solution)/shard_map/cond/branch_0_fun/ppermute | solution.py:33
  222.0 11.1 %collective-permute-done.31.refs_1_ = bf16[128,2048]{1,0:T(8,128)(2,1)S(1)} collective-permute-done((bf16[128,2048]{1,0:T(8,128)(2,1)S(1)}, bf16[128,2048]{1,0:T(8,128)(2,1)S(1)}, u32[]{:S(2)}, u32[]{:S(2)}) %collective-permute-start.31) | collective-permute-done | bytes 524320 | tf_op jit(solution)/shard_map/cond/branch_0_fun/ppermute | solution.py:25
  234.7 14.6 %collective-permute-done.36.refs_2_ = bf16[128,2048]{1,0:T(8,128)(2,1)S(1)} collective-permute-done((bf16[128,2048]{1,0:T(8,128)(2,1)S(1)}, bf16[128,2048]{1,0:T(8,128)(2,1)S(1)}, u32[]{:S(2)}, u32[]{:S(2)}) %collective-permute-start.36) | collective-permute-done | bytes 524320 | tf_op jit(solution)/shard_map/cond/branch_0_fun/ppermute | solution.py:25
  254.5 8.0 %collective-permute-done.37.peer = bf16[2,256,768]{2,1,0:T(8,128)(2,1)S(1)} collective-permute-done((bf16[2,256,768]{2,1,0:T(8,128)(2,1)}, bf16[2,256,768]{2,1,0:T(8,128)(2,1)S(1)}, u32[]{:S(2)}, u32[]{:S(2)}) %collective-permute-start.37) | collective-permute-done | bytes 786464 | tf_op jit(solution)/shard_map/cond/branch_0_fun/ppermute | solution.py:38
  (138 shorter events, 75.8 us)
Async XLA Ops:
  1.3 30.5 %collective-permute-start = (bf16[128,2048]{1,0:T(8,128)(2,1)}, bf16[128,2048]{1,0:T(8,128)(2,1)S(1)}, u32[]{:S(2)}, u32[]{:S(2)}) collective-permute-start(bf16[128,2048]{1,0:T(8,128)(2,1)} %get-tuple-element.52.value.refs_0_.base), channel_id=1, source_target_pairs={{0,2},{1,3},{2,0},{3,1},{4,6},{5,7},{6,4},{7,5},{8,10},{9,11},{10,... | collective-permute-start | bytes 1572872 | tf_op jit(solution)/shard_map/cond/branch_0_fun/ppermute | solution.py:25
  4.4 27.4 %collective-permute-start.1 = (bf16[128,2048]{1,0:T(8,128)(2,1)}, bf16[128,2048]{1,0:T(8,128)(2,1)S(1)}, u32[]{:S(2)}, u32[]{:S(2)}) collective-permute-start(bf16[128,2048]{1,0:T(8,128)(2,1)} %get-tuple-element.52.value.refs_0_.base), channel_id=1, source_target_pairs={{0,6},{1,7},{2,4},{3,5},{4,2},{5,3},{6,0},{7,1},{8,14},{9,15},{10,... | collective-permute-start | bytes 1572872 | tf_op jit(solution)/shard_map/cond/branch_0_fun/ppermute | solution.py:25
  6.9 13.3 %collective-permute-start.2 = (bf16[128,2048]{1,0:T(8,128)(2,1)}, bf16[128,2048]{1,0:T(8,128)(2,1)S(1)}, u32[]{:S(2)}, u32[]{:S(2)}) collective-permute-start(bf16[128,2048]{1,0:T(8,128)(2,1)} %get-tuple-element.71.value.refs_0_.base), channel_id=1, source_target_pairs={{0,8},{8,0},{16,24},{24,16},{1,9},{9,1},{17,25},{25,17},{2,10},{10... | collective-permute-start | bytes 1572872 | tf_op jit(solution)/shard_map/cond/branch_0_fun/ppermute | solution.py:38
  32.8 13.5 %collective-permute-start.5 = (bf16[2,64,2048]{2,1,0:T(8,128)(2,1)}, bf16[2,64,2048]{2,1,0:T(8,128)(2,1)S(1)}, u32[]{:S(2)}, u32[]{:S(2)}) collective-permute-start(bf16[2,64,2048]{2,1,0:T(8,128)(2,1)} %get-tuple-element.49), channel_id=1, source_target_pairs={{0,8},{8,0},{16,24},{24,16},{1,9},{9,1},{17,25},{25,17},{2,10},{10... | collective-permute-start | bytes 1572872 | tf_op jit(solution)/shard_map/cond/branch_0_fun/ppermute | solution.py:38
  34.4 12.8 %collective-permute-start.4 = (bf16[128,2048]{1,0:T(8,128)(2,1)S(1)}, bf16[128,2048]{1,0:T(8,128)(2,1)S(1)}, u32[]{:S(2)}, u32[]{:S(2)}) collective-permute-start(bf16[128,2048]{1,0:T(8,128)(2,1)S(1)} %branch_0_fun.22), channel_id=1, source_target_pairs={{0,4},{1,5},{2,0},{3,1},{4,6},{5,7},{6,2},{7,3},{8,12},{9,13},{10,... | collective-permute-start | bytes 1572872 | tf_op jit(solution)/shard_map/cond/branch_0_fun/ppermute | solution.py:33
  47.2 29.5 %collective-permute-start.13 = (bf16[2,144,2048]{2,1,0:T(8,128)(2,1)}, bf16[2,144,2048]{2,1,0:T(8,128)(2,1)S(1)}, u32[]{:S(2)}, u32[]{:S(2)}) collective-permute-start(bf16[2,144,2048]{2,1,0:T(8,128)(2,1)} %get-tuple-element.63), channel_id=1, source_target_pairs={{0,8},{8,0},{16,24},{24,16},{1,9},{9,1},{17,25},{25,17},{2,10},{10... | collective-permute-start | bytes 3538952 | tf_op jit(solution)/shard_map/cond/branch_0_fun/ppermute | solution.py:38
  50.1 18.7 %collective-permute-start.11 = (bf16[128,2048]{1,0:T(8,128)(2,1)}, bf16[128,2048]{1,0:T(8,128)(2,1)S(1)}, u32[]{:S(2)}, u32[]{:S(2)}) collective-permute-start(bf16[128,2048]{1,0:T(8,128)(2,1)} %get-tuple-element.71.value.refs_0_.base), channel_id=1, source_target_pairs={{0,2},{1,3},{2,0},{3,1},{4,6},{5,7},{6,4},{7,5},{8,10},{9,11},{10,... | collective-permute-start | bytes 1572872 | tf_op jit(solution)/shard_map/cond/branch_0_fun/ppermute | solution.py:25
  51.0 25.7 %collective-permute-start.12 = (bf16[128,2048]{1,0:T(8,128)(2,1)}, bf16[128,2048]{1,0:T(8,128)(2,1)S(1)}, u32[]{:S(2)}, u32[]{:S(2)}) collective-permute-start(bf16[128,2048]{1,0:T(8,128)(2,1)} %get-tuple-element.71.value.refs_0_.base), channel_id=1, source_target_pairs={{0,6},{1,7},{2,4},{3,5},{4,2},{5,3},{6,0},{7,1},{8,14},{9,15},{10,... | collective-permute-start | bytes 1572872 | tf_op jit(solution)/shard_map/cond/branch_0_fun/ppermute | solution.py:25
  77.1 20.0 %collective-permute-start.16 = (bf16[2,512,384]{2,1,0:T(8,128)(2,1)S(1)}, bf16[2,512,384]{2,1,0:T(8,128)(2,1)S(1)}, u32[]{:S(2)}, u32[]{:S(2)}) collective-permute-start(bf16[2,512,384]{2,1,0:T(8,128)(2,1)S(1)} %get-tuple-element.70.left.refs_9_), channel_id=1, source_target_pairs={{0,8},{8,0},{16,24},{24,16},{1,9},{9,1},{17,25},{25,17},{2,10},{10... | collective-permute-start | bytes 2359304 | tf_op jit(solution)/shard_map/cond/branch_0_fun/ppermute | solution.py:38
  78.3 14.0 %collective-permute-start.14 = (bf16[128,2048]{1,0:T(8,128)(2,1)S(1)}, bf16[128,2048]{1,0:T(8,128)(2,1)S(1)}, u32[]{:S(2)}, u32[]{:S(2)}) collective-permute-start(bf16[128,2048]{1,0:T(8,128)(2,1)S(1)} %branch_0_fun.25), channel_id=1, source_target_pairs={{0,4},{1,5},{2,0},{3,1},{4,6},{5,7},{6,2},{7,3},{8,12},{9,13},{10,... | collective-permute-start | bytes 1572872 | tf_op jit(solution)/shard_map/cond/branch_0_fun/ppermute | solution.py:33
  97.9 22.4 %collective-permute-start.21 = (bf16[2,112,2048]{2,1,0:T(8,128)(2,1)S(1)}, bf16[2,112,2048]{2,1,0:T(8,128)(2,1)S(1)}, u32[]{:S(2)}, u32[]{:S(2)}) collective-permute-start(bf16[2,112,2048]{2,1,0:T(8,128)(2,1)S(1)} %copy-done.48), channel_id=1, source_target_pairs={{0,8},{8,0},{16,24},{24,16},{1,9},{9,1},{17,25},{25,17},{2,10},{10... | collective-permute-start | bytes 2752520 | tf_op jit(solution)/shard_map/cond/branch_0_fun/ppermute | solution.py:38
  121.3 24.0 %collective-permute-start.24 = (bf16[128,2048]{1,0:T(8,128)(2,1)S(1)}, bf16[128,2048]{1,0:T(8,128)(2,1)S(1)}, u32[]{:S(2)}, u32[]{:S(2)}) collective-permute-start(bf16[128,2048]{1,0:T(8,128)(2,1)S(1)} %get-tuple-element.92), channel_id=1, source_target_pairs={{0,2},{1,3},{2,6},{3,7},{4,0},{5,1},{6,4},{7,5},{8,10},{9,11},{10,... | collective-permute-start | bytes 1572872 | tf_op jit(solution)/shard_map/cond/branch_0_fun/ppermute | solution.py:33
  121.3 26.0 %collective-permute-start.25 = (bf16[128,2048]{1,0:T(8,128)(2,1)S(1)}, bf16[128,2048]{1,0:T(8,128)(2,1)S(1)}, u32[]{:S(2)}, u32[]{:S(2)}) collective-permute-start(bf16[128,2048]{1,0:T(8,128)(2,1)S(1)} %get-tuple-element.93), channel_id=1, source_target_pairs={{0,2},{1,3},{2,0},{3,1},{4,6},{5,7},{6,4},{7,5},{8,10},{9,11},{10,... | collective-permute-start | bytes 1572872 | tf_op jit(solution)/shard_map/cond/branch_0_fun/ppermute | solution.py:25
  123.2 34.6 %collective-permute-start.22 = (bf16[128,2048]{1,0:T(8,128)(2,1)S(1)}, bf16[128,2048]{1,0:T(8,128)(2,1)S(1)}, u32[]{:S(2)}, u32[]{:S(2)}) collective-permute-start(bf16[128,2048]{1,0:T(8,128)(2,1)S(1)} %collective-permute-done.2.value.refs_0_), channel_id=1, source_target_pairs={{0,2},{1,3},{2,0},{3,1},{4,6},{5,7},{6,4},{7,5},{8,10},{9,11},{10,... | collective-permute-start | bytes 1572872 | tf_op jit(solution)/shard_map/cond/branch_0_fun/ppermute | solution.py:25
  123.3 46.4 %collective-permute-start.23 = (bf16[128,2048]{1,0:T(8,128)(2,1)S(1)}, bf16[128,2048]{1,0:T(8,128)(2,1)S(1)}, u32[]{:S(2)}, u32[]{:S(2)}) collective-permute-start(bf16[128,2048]{1,0:T(8,128)(2,1)S(1)} %collective-permute-done.2.value.refs_0_), channel_id=1, source_target_pairs={{0,6},{1,7},{2,4},{3,5},{4,2},{5,3},{6,0},{7,1},{8,14},{9,15},{10,... | collective-permute-start | bytes 1572872 | tf_op jit(solution)/shard_map/cond/branch_0_fun/ppermute | solution.py:25
  126.1 54.2 %collective-permute-start.28 = (bf16[2,768,768]{2,1,0:T(8,128)(2,1)S(1)}, bf16[2,768,768]{2,1,0:T(8,128)(2,1)S(1)}, u32[]{:S(2)}, u32[]{:S(2)}) collective-permute-start(bf16[2,768,768]{2,1,0:T(8,128)(2,1)S(1)} %get-tuple-element.102.own), channel_id=1, source_target_pairs={{0,8},{8,0},{16,24},{24,16},{1,9},{9,1},{17,25},{25,17},{2,10},{10... | collective-permute-start | bytes 7077896 | tf_op jit(solution)/shard_map/cond/branch_0_fun/ppermute | solution.py:38
  170.1 80.9 %collective-permute-start.38 = (bf16[2,1024,768]{2,1,0:T(8,128)(2,1)S(1)}, bf16[2,1024,768]{2,1,0:T(8,128)(2,1)S(1)}, u32[]{:S(2)}, u32[]{:S(2)}) collective-permute-start(bf16[2,1024,768]{2,1,0:T(8,128)(2,1)S(1)} %get-tuple-element.122.own), channel_id=1, source_target_pairs={{0,8},{8,0},{16,24},{24,16},{1,9},{9,1},{17,25},{25,17},{2,10},{10... | collective-permute-start | bytes 9437192 | tf_op jit(solution)/shard_map/cond/branch_0_fun/ppermute | solution.py:38
  171.4 16.7 %collective-permute-start.29 = (bf16[128,2048]{1,0:T(8,128)(2,1)S(1)}, bf16[128,2048]{1,0:T(8,128)(2,1)S(1)}, u32[]{:S(2)}, u32[]{:S(2)}) collective-permute-start(bf16[128,2048]{1,0:T(8,128)(2,1)S(1)} %branch_0_fun.35), channel_id=1, source_target_pairs={{0,6},{1,7},{2,4},{3,5},{4,2},{5,3},{6,0},{7,1},{8,14},{9,15},{10,... | collective-permute-start | bytes 1572872 | tf_op jit(solution)/shard_map/cond/branch_0_fun/ppermute | solution.py:25
  173.1 24.9 %collective-permute-start.27 = (bf16[128,2048]{1,0:T(8,128)(2,1)S(1)}, bf16[128,2048]{1,0:T(8,128)(2,1)S(1)}, u32[]{:S(2)}, u32[]{:S(2)}) collective-permute-start(bf16[128,2048]{1,0:T(8,128)(2,1)S(1)} %branch_0_fun.32), channel_id=1, source_target_pairs={{0,4},{1,5},{2,0},{3,1},{4,6},{5,7},{6,2},{7,3},{8,12},{9,13},{10,... | collective-permute-start | bytes 1572872 | tf_op jit(solution)/shard_map/cond/branch_0_fun/ppermute | solution.py:33
  198.6 12.6 %collective-permute-start.35 = (bf16[128,2048]{1,0:T(8,128)(2,1)S(1)}, bf16[128,2048]{1,0:T(8,128)(2,1)S(1)}, u32[]{:S(2)}, u32[]{:S(2)}) collective-permute-start(bf16[128,2048]{1,0:T(8,128)(2,1)S(1)} %collective-permute-done.23.far.refs_6_), channel_id=1, source_target_pairs={{0,1},{1,0},{2,3},{3,2},{4,5},{5,4},{6,7},{7,6},{8,9},{9,8},{10,11... | collective-permute-start | bytes 1572872 | tf_op jit(solution)/shard_map/cond/branch_0_fun/ppermute | solution.py:25
  200.0 22.0 %collective-permute-start.30 = (bf16[128,2048]{1,0:T(8,128)(2,1)S(1)}, bf16[128,2048]{1,0:T(8,128)(2,1)S(1)}, u32[]{:S(2)}, u32[]{:S(2)}) collective-permute-start(bf16[128,2048]{1,0:T(8,128)(2,1)S(1)} %copy-done.29), channel_id=1, source_target_pairs={{0,2},{1,3},{2,6},{3,7},{4,0},{5,1},{6,4},{7,5},{8,10},{9,11},{10,... | collective-permute-start | bytes 1572872 | tf_op jit(solution)/shard_map/cond/branch_0_fun/ppermute | solution.py:33
  208.5 24.6 %collective-permute-start.31 = (bf16[128,2048]{1,0:T(8,128)(2,1)S(1)}, bf16[128,2048]{1,0:T(8,128)(2,1)S(1)}, u32[]{:S(2)}, u32[]{:S(2)}) collective-permute-start(bf16[128,2048]{1,0:T(8,128)(2,1)S(1)} %copy-done.25), channel_id=1, source_target_pairs={{0,2},{1,3},{2,0},{3,1},{4,6},{5,7},{6,4},{7,5},{8,10},{9,11},{10,... | collective-permute-start | bytes 1572872 | tf_op jit(solution)/shard_map/cond/branch_0_fun/ppermute | solution.py:25
  209.2 53.3 %collective-permute-start.37 = (bf16[2,256,768]{2,1,0:T(8,128)(2,1)}, bf16[2,256,768]{2,1,0:T(8,128)(2,1)S(1)}, u32[]{:S(2)}, u32[]{:S(2)}) collective-permute-start(bf16[2,256,768]{2,1,0:T(8,128)(2,1)} %get-tuple-element.86.own), channel_id=1, source_target_pairs={{0,8},{8,0},{16,24},{24,16},{1,9},{9,1},{17,25},{25,17},{2,10},{10... | collective-permute-start | bytes 2359304 | tf_op jit(solution)/shard_map/cond/branch_0_fun/ppermute | solution.py:38
  233.4 15.8 %collective-permute-start.36 = (bf16[128,2048]{1,0:T(8,128)(2,1)S(1)}, bf16[128,2048]{1,0:T(8,128)(2,1)S(1)}, u32[]{:S(2)}, u32[]{:S(2)}) collective-permute-start(bf16[128,2048]{1,0:T(8,128)(2,1)S(1)} %branch_0_fun.38), channel_id=1, source_target_pairs={{0,6},{1,7},{2,4},{3,5},{4,2},{5,3},{6,0},{7,1},{8,14},{9,15},{10,... | collective-permute-start | bytes 1572872 | tf_op jit(solution)/shard_map/cond/branch_0_fun/ppermute | solution.py:25
  (41 other events, 495.7 us)
where the time goes:
time: 265 us
  waiting for transfers between devices  134 us (51%)
  Pallas kernels  77 us (29%)
  starting transfers between devices  45 us (17%)
  local copies, waits for them, and re-layouts  6.54 us (2%)
    pallas_call x21, Pallas kernels, kernel_call(): pl.pallas_call(body, grid=grid, in_specs=[spec(b, w) for _, b, w in ins],...  77 us
    ppermute x24, waiting for transfers between devices, to_xor(): return lax.ppermute(value, 'exp', [(i, i ^ k) for i in range(size)])  70.6 us
    ppermute x10, waiting for transfers between devices, gossip(): return lax.ppermute(value, 'rep', [(i, i ^ 1 << bit) for i in range(size)])  33.5 us
    ppermute x5, waiting for transfers between devices, along_chips(): lax.ppermute(value, 'exp', [(2 * c + k, 2 * t + k) for c, t in enumerate(...  23.9 us
    ppermute x24, starting transfers between devices, to_xor(): return lax.ppermute(value, 'exp', [(i, i ^ k) for i in range(size)])  20.4 us
    ppermute x10, starting transfers between devices, gossip(): return lax.ppermute(value, 'rep', [(i, i ^ 1 << bit) for i in range(size)])  10.8 us
    ppermute x5, starting transfers between devices, along_chips(): lax.ppermute(value, 'exp', [(2 * c + k, 2 * t + k) for c, t in enumerate(...  10.5 us
    all_to_all x1, waiting for transfers between devices, routing(): lax.all_to_all(packed, 'exp', split_axis=0, concat_axis=0, tiled=True)  5.54 us
  transfers between devices with their start and end apart: 40, of which 25 were waited for; matrix products, arithmetic and copies ran while one was open for 1% of the time, Pallas kernels for 28%

commit v1 on v0

--- a/solution.py
+++ b/solution.py
@@ -14,7 +14,7 @@
 COLS = 512
 DEEP = 256
 SCALARS = ()
-PIECES = (4, 4, 9, 7)
+PIECES = (4, 4, 11, 5)
 F32 = jnp.float32
 BF16 = jnp.bfloat16
 VMEM = 32 * 1024 * 1024
@@ -137,11 +137,12 @@
 
 
 def forward_body(groups, local, hidden, scale, *refs):
-    blocks, (mine, w, rows, inner, slope, value, joint) = refs[:groups], refs[groups:]
+    blocks, (mine, w, turned, inner, turned_inner, slope, value, joint, rows) = refs[:groups], refs[groups:]
     fill_rows(blocks, mine, rows, local, False)
     first = pl.program_id(0) == 0
 
     for a in range(local):
+        turned[a] = rows[a].T
         part = nn(rows[a], w[a])
 
         @pl.when(first)
@@ -160,6 +161,7 @@
             sigmoid = jax.nn.sigmoid(gate)
             act = gate * sigmoid
             inner[a] = (act * upper).astype(BF16)
+            turned_inner[a] = inner[a].T
             slope[a] = upper * (sigmoid * (1.0 + gate * (1.0 - sigmoid)))
             value[a] = act
 
@@ -175,24 +177,25 @@
         [(b, (tokens, COLS), lambda j: (0, j)) for b in blocks]
         + [(mine, mine.shape, whole), (proj_in, (local, COLS, double), lambda j: (0, j, 0))],
         [
-            (shape((local, rows, width), BF16), (local, rows, COLS), lambda j: (0, 0, j)),
+            (shape((local, width, rows), BF16), (local, COLS, rows), lambda j: (0, j, 0)),
             (shape((local, rows, hidden), BF16), (local, rows, hidden), whole),
+            (shape((local, hidden, rows), BF16), (local, hidden, rows), whole),
             (shape((local, rows, hidden), F32), (local, rows, hidden), whole),
             (shape((local, rows, hidden), F32), (local, rows, hidden), whole),
         ],
-        [pltpu.VMEM((local, rows, double), F32)],
+        [pltpu.VMEM((local, rows, double), F32), pltpu.VMEM((local, rows, COLS), BF16)],
         2 * local * rows * width * double,
     )
 
 
 def backward_body(groups, local, hidden, scale, *refs):
     blocks = refs[:groups]
-    mine, inner, slope, value, w, mom, new_mom, update, grad_joint, rows, grad_inner = refs[groups:]
+    mine, turned_inner, slope, value, w, mom, new_mom, update, grad_joint, rows, grad_inner = refs[groups:]
     fill_rows(blocks, mine, rows, local, True)
     first = pl.program_id(0) == 0
 
     for a in range(local):
-        moment = MOMENTUM_DECAY * mom[a].astype(F32) + tn(inner[a], rows[a]) * scale
+        moment = MOMENTUM_DECAY * mom[a].astype(F32) + nn(turned_inner[a], rows[a]) * scale
         new_mom[a] = moment.astype(BF16)
         update[a] = (w[a].astype(F32) - STEP_SIZE * moment).astype(BF16)
         part = nt(rows[a], w[a])
@@ -213,7 +216,7 @@
             grad_joint[a, :, hidden:] = (grad * value[a]).astype(BF16)
 
 
-def backward(blocks, mine, inner, slope, value, proj_out, mom_out):
+def backward(blocks, mine, turned_inner, slope, value, proj_out, mom_out):
     groups = len(blocks)
     local, hidden, width = proj_out.shape
     rows, tokens = groups * CAP, blocks[0].shape[0]
@@ -224,7 +227,7 @@
         partial(backward_body, groups, local, hidden, 1.0 / math.sqrt(hidden)),
         (width // COLS,),
         [(b, (tokens, COLS), lambda j: (0, j)) for b in blocks]
-        + [(mine, mine.shape, whole), (inner, *held), (slope, *held), (value, *held), (proj_out, *cut), (mom_out, *cut)],
+        + [(mine, mine.shape, whole), (turned_inner, (local, hidden, rows), whole), (slope, *held), (value, *held), (proj_out, *cut), (mom_out, *cut)],
         [
             (proj_out, *cut),
             (proj_out, *cut),
@@ -237,15 +240,15 @@
 
 
 def peer_body(groups, local, scale, *refs):
-    blocks, (mine, inner, *bases, update, new_w, rows) = refs[:groups], refs[groups:]
+    blocks, (mine, turned_inner, *bases, update, new_w, rows) = refs[:groups], refs[groups:]
     fill_rows(blocks, mine, rows, local, True)
     for a in range(local):
         whole = jnp.concatenate([base[a].astype(F32) for base in bases], axis=0)
-        theirs = whole - STEP_SIZE * (tn(inner[a], rows[a]) * scale)
+        theirs = whole - STEP_SIZE * (nn(turned_inner[a], rows[a]) * scale)
         new_w[a] = (0.5 * (update[a].astype(F32) + theirs)).astype(BF16)
 
 
-def peer_out(blocks, mine, inner, bases, update):
+def peer_out(blocks, mine, turned_inner, bases, update):
     groups = len(blocks)
     local, hidden, width = update.shape
     rows, tokens = groups * CAP, blocks[0].shape[0]
@@ -255,7 +258,7 @@
         partial(peer_body, groups, local, 1.0 / math.sqrt(hidden)),
         (width // COLS,),
         [(b, (tokens, COLS), lambda j: (0, j)) for b in blocks]
-        + [(mine, mine.shape, whole), (inner, (local, rows, hidden), whole)]
+        + [(mine, mine.shape, whole), (turned_inner, (local, hidden, rows), whole)]
         + [(b, (local, b.shape[1], COLS), lambda j: (0, 0, j)) for b in bases]
         + [(update, *cut)],
         [(update, *cut)],
@@ -282,20 +285,20 @@
     return kernel_call(base_body, (width // COLS,), [(proj_out, *cut), (mom_out, *cut)], outs, kept=kept)
 
 
-def grad_in_body(scale, rows, grad_joint, w, mom, *rest):
+def grad_in_body(scale, turned, grad_joint, w, mom, *rest):
     update, new_mom = rest[-2:]
-    moment = MOMENTUM_DECAY * mom[0].astype(F32) + tn(rows[0], grad_joint[0]) * scale
+    moment = MOMENTUM_DECAY * mom[0].astype(F32) + nn(turned[0], grad_joint[0]) * scale
     new_mom[0] = moment.astype(BF16)
     update[0] = (w[0].astype(F32) - STEP_SIZE * moment).astype(BF16)
 
 
-def grad_in(rows_in, grad_joint, proj_in, mom_in, start, depth, held):
+def grad_in(turned_rows, grad_joint, proj_in, mom_in, start, depth, held):
     local, width, double = proj_in.shape
-    rows = rows_in.shape[1]
+    rows = turned_rows.shape[2]
     first = start // DEEP
     cut = ((1, DEEP, double), lambda a, i: (a, first + i, 0))
     ins = [
-        (rows_in, (1, rows, DEEP), lambda a, i: (a, 0, first + i)),
+        (turned_rows, (1, DEEP, rows), lambda a, i: (a, first + i, 0)),
         (grad_joint, (1, rows, double), lambda a, i: (a, 0, 0)),
         (proj_in, *cut),
         (mom_in, *cut),
@@ -462,27 +465,29 @@
     upstream_now, base = ties((upstream, bases[2], *tok_same[1:], peer_bases[1]))[:2]
     cot = near_and_far(upstream_now)
     peer_bases.append(gossip(base, bit))
-    rows_in, inner, slope, value = forward(with_other_core(tok_same), mine, proj_in)
+    turned_rows, inner, turned_inner, slope, value = forward(with_other_core(tok_same), mine, proj_in)
     own, other = returns(inner, proj_out, mine, True)
     *cot, own, peer_bases[2] = ties((*cot, own, peer_bases[2]))
     sent = middle_of(upstream, cot, ends)
     cot_same = all_blocks(upstream, cot, sent)
-    peer_inner = gossip(after(inner, sent), bit)
+    peer_bases.append(gossip(after(bases[3], sent), bit))
     total_1, parts_1 = paired(inputs, own, after(other, sent))
 
-    *cot_same, total_1, peer_inner = ties((*cot_same, total_1, peer_inner))
-    peer_bases.append(gossip(after(bases[3], peer_inner), bit))
-    cot_all = with_other_core(cot_same)
-    new_mom_out, update_out, grad_joint = backward(cot_all, mine, inner, slope, value, proj_out, mom_out)
-    update_0, new_mom_in = grad_in(rows_in, grad_joint, proj_in, mom_in, 0, first_rows, None)
+    early = [0, 1, 3] if len(cot_same) == 4 else []
+    swapped = {s: swap(cot_same[s]) for s in early}
+    *cot_same, total_1, peer_bases[3], swapped = ties((*cot_same, total_1, peer_bases[3], swapped))
+    peer_inner = gossip(after(turned_inner, peer_bases[3]), bit)
+    cot_all = [part for s, block in enumerate(cot_same) for part in (block, swapped[s] if s in swapped else swap(block))]
+    new_mom_out, update_out, grad_joint = backward(cot_all, mine, turned_inner, slope, value, proj_out, mom_out)
+    update_0, new_mom_in = grad_in(turned_rows, grad_joint, proj_in, mom_in, 0, first_rows, None)
     peer_0 = gossip(update_0, bit)
-    peer_upstream, new_mom_in, peer_bases[3] = ties((peer_upstream, new_mom_in, peer_bases[3]))
-    heard_1 = send_first(parts_1, new_mom_in)
-    there = near_and_far(peer_upstream)
+    new_mom_in, peer_inner = ties((new_mom_in, peer_inner))
+    heard_1 = send_first(parts_1, cot_same[2])
+    there = near_and_far(after(peer_upstream, cot_same[2]))
     last = width - DEEP
-    update_1, new_mom_in = grad_in(rows_in, grad_joint, proj_in, mom_in, first_rows, last - first_rows, new_mom_in)
+    update_1, new_mom_in = grad_in(turned_rows, grad_joint, proj_in, mom_in, first_rows, last - first_rows, new_mom_in)
     peer_1 = gossip(update_1, bit)
-    update_2, new_mom_in = grad_in(rows_in, grad_joint, proj_in, mom_in, last, DEEP, new_mom_in)
+    update_2, new_mom_in = grad_in(turned_rows, grad_joint, proj_in, mom_in, last, DEEP, new_mom_in)
     peer_2 = gossip(update_2, bit)
     own, other = returns(after(grad_joint, update_2), proj_in, mine, False)
 

time: 265 us -> 259 us (0.977)
  local copies, waits for them, and re-layouts: 6.54 us -> 3.01 us
  waiting for transfers between devices: 134 us -> 131 us
    ppermute x10, waiting for transfers between devices: 33.5 us -> 68.2 us  [gossip(): return lax.ppermute(value, 'rep', [(i, i ^ 1 << bit) for i in range(size)])]
    ppermute x24, waiting for transfers between devices: 70.6 us -> 44.3 us  [to_xor(): return lax.ppermute(value, 'exp', [(i, i ^ k) for i in range(size)])]
    ppermute x5, waiting for transfers between devices: 23.9 us -> 12.9 us  [along_chips(): lax.ppermute(value, 'exp', [(2 * c + k, 2 * t + k) for c, t in enumerate(...]
    cond x50 -> x30, local copies, waits for them, and re-layouts: 5.35 us -> 1.82 us
  transfers between devices with their start and end apart: 40 -> 40, of which waited for: 25 -> 19; matrix products, arithmetic and copies ran while one was open for 1% -> 1% of each run, Pallas kernels for 28% -> 29%
where the time goes in v1:
time: 259 us
  waiting for transfers between devices  131 us (51%)
  Pallas kernels  77.2 us (30%)
  starting transfers between devices  45.1 us (17%)
  local copies, waits for them, and re-layouts  3.01 us (1%)
    pallas_call x21, Pallas kernels, kernel_call(): pl.pallas_call(body, grid=grid, in_specs=[spec(b, w) for _, b, w in ins],...  77.2 us
    ppermute x10, waiting for transfers between devices, gossip(): return lax.ppermute(value, 'rep', [(i, i ^ 1 << bit) for i in range(size)])  68.2 us
    ppermute x24, waiting for transfers between devices, to_xor(): return lax.ppermute(value, 'exp', [(i, i ^ k) for i in range(size)])  44.3 us
    ppermute x24, starting transfers between devices, to_xor(): return lax.ppermute(value, 'exp', [(i, i ^ k) for i in range(size)])  20.1 us
    ppermute x5, waiting for transfers between devices, along_chips(): lax.ppermute(value, 'exp', [(2 * c + k, 2 * t + k) for c, t in enumerate(...  12.9 us
    ppermute x5, starting transfers between devices, along_chips(): lax.ppermute(value, 'exp', [(2 * c + k, 2 * t + k) for c, t in enumerate(...  11.1 us
    ppermute x10, starting transfers between devices, gossip(): return lax.ppermute(value, 'rep', [(i, i ^ 1 << bit) for i in range(size)])  10.5 us
    all_to_all x1, waiting for transfers between devices, routing(): lax.all_to_all(packed, 'exp', split_axis=0, concat_axis=0, tiled=True)  5.54 us
  transfers between devices with their start and end apart: 40, of which 19 were waited for; matrix products, arithmetic and copies ran while one was open for 1% of the time, Pallas kernels for 29%

profile of v1, /device:TPU:0, one launch (start us, length us, event | category | flops | bytes accessed | tf_op | source)
XLA Modules:
  0.0 258.8 jit_solution(11837730522386716355)
XLA Ops:
  1.3 257.5 %conditional.1 = (bf16[1,128,2048]{2,1,0:T(8,128)(2,1)}, bf16[1,128,2048]{2,1,0:T(8,128)(2,1)}, bf16[1,2,2048,768]{3,2,1,0:T(8,128)(2,1)}, bf16[1,2,384,2048]{3,...) conditional(s32[]{:T(128)} %clamp.3, (bf16[128,2048]{1,0:T(8,128)(2,1)}, ...), branch_computations={%region_0.3_spmd, %region_3.6_spmd} | conditional | flops 5368847360 | bytes 236377312 | solution.py:518
  9.3 5.0 %branch_1_fun.21 = (bf16[2,64,2048]{2,1,0:T(8,128)(2,1)}, bf16[2,64,2048]{2,1,0:T(8,128)(2,1)}, bf16[2,176,2048]{2,1,0:T(8,128)(2,1)}, bf16[2,80,2048]{2,1,0:T(8,128)(2,1)}) custom-call(bf16[2,384,2048]{2,1,0:T(8,128)(2,1)} %get-tuple-element.137.w.refs_12_, bf16[2,384,2048]{2,1,0:T(8,128)(2,1)} %get-tuple-element.138.mom.refs_13_), custom_call_target="tpu_custom_call" | custom-call | bytes 3145728 | tf_op jit(solution)/shard_map/cond/branch_1_fun/pallas_call | solution.py:93
  14.5 5.9 %collective-permute-done.41.value.refs_0_ = bf16[128,2048]{1,0:T(8,128)(2,1)S(1)} collective-permute-done((bf16[128,2048]{1,0:T(8,128)(2,1)}, bf16[128,2048]{1,0:T(8,128)(2,1)S(1)}, u32[]{:S(2)}, u32[]{:S(2)}) %collective-permute-start.41) | collective-permute-done | bytes 524320 | tf_op jit(solution)/shard_map/cond/branch_1_fun/ppermute | solution.py:38
  22.6 3.3 %all-to-all-start.1 = ((f32[8,4,128]{2,1,0:T(4,128)}), f32[8,4,128]{2,1,0:T(4,128)S(1)}, u32[]{:S(2)}, u32[]{:S(2)}) async-start(f32[8,4,128]{2,1,0:T(4,128)} %bitcast.21), calls=%async_computation.1 | async-start | bytes 32768 | tf_op jit(solution)/shard_map/cond/branch_1_fun/all_to_all | solution.py:441
  26.0 5.5 %all-to-all-done.1 = f32[8,4,128]{2,1,0:T(4,128)S(1)} async-done(((f32[8,4,128]{2,1,0:T(4,128)}), f32[8,4,128]{2,1,0:T(4,128)S(1)}, u32[]{:S(2)}, u32[]{:S(2)}) %all-to-all-start.1) | async-done | bytes 16416 | tf_op jit(solution)/shard_map/cond/branch_1_fun/all_to_all | solution.py:441
  35.9 10.8 %collective-permute-done.45.refs_8_ = f32[8,4,128]{2,1,0:T(4,128)S(1)} collective-permute-done((f32[8,4,128]{2,1,0:T(4,128)S(1)}, f32[8,4,128]{2,1,0:T(4,128)S(1)}, u32[]{:S(2)}, u32[]{:S(2)}) %collective-permute-start.45) | collective-permute-done | bytes 16416 | tf_op jit(solution)/shard_map/cond/branch_1_fun/ppermute | solution.py:38
  53.5 10.8 %branch_1_fun.23 = (bf16[2,2048,512]{2,1,0:T(8,128)(2,1)S(1)}, bf16[2,512,384]{2,1,0:T(8,128)(2,1)S(1)}, bf16[2,384,512]{2,1,0:T(8,128)(2,1)S(1)}, f32[2,512,384]{2,1,0:T(8,128)S(1)}, f32[2,512,384]{2,1,0:T(8,128)S(1)}) custom-call(bf16[128,2048]{1,0:T(8,128)(2,1)S(1)} %copy-done.19, bf16[128,2048]{1,0:T(8,128)(2,1)S(1)} %collective-permute-done.48.refs_1_, ...), custom_call_target="tpu_custom_call" | custom-call | flops 1073741824 | bytes 6471680 | tf_op jit(solution)/shard_map/cond/branch_1_fun/pallas_call | solution.py:93
  64.4 4.6 %branch_1_fun.24 = (f32[4,128,2048]{2,1,0:T(8,128)S(1)}, bf16[4,128,2048]{2,1,0:T(8,128)(2,1)S(1)}) custom-call(bf16[2,512,384]{2,1,0:T(8,128)(2,1)S(1)} %get-tuple-element.156.left, bf16[2,384,2048]{2,1,0:T(8,128)(2,1)S(1)} %copy-done.17, f32[8,4,128]{2,1,0:T(4,128)S(1)} %gather_fusion.1), custom_call_target="tpu_custom_call" | custom-call | flops 536870912 | bytes 3413333 | tf_op jit(solution)/shard_map/cond/branch_1_fun/pallas_call | solution.py:93
  69.0 7.8 %collective-permute-done.47.far.refs_6_ = bf16[128,2048]{1,0:T(8,128)(2,1)S(1)} collective-permute-done((bf16[128,2048]{1,0:T(8,128)(2,1)S(1)}, bf16[128,2048]{1,0:T(8,128)(2,1)S(1)}, u32[]{:S(2)}, u32[]{:S(2)}) %collective-permute-start.47) | collective-permute-done | bytes 524320 | tf_op jit(solution)/shard_map/cond/branch_1_fun/ppermute | solution.py:25
  86.0 8.7 %collective-permute-done.53.refs_4_ = bf16[128,2048]{1,0:T(8,128)(2,1)S(1)} collective-permute-done((bf16[128,2048]{1,0:T(8,128)(2,1)S(1)}, bf16[128,2048]{1,0:T(8,128)(2,1)S(1)}, u32[]{:S(2)}, u32[]{:S(2)}) %collective-permute-start.53) | collective-permute-done | bytes 524320 | tf_op jit(solution)/shard_map/cond/branch_1_fun/ppermute | solution.py:33
  103.5 10.4 %branch_1_fun.27 = (bf16[2,384,2048]{2,1,0:T(8,128)(2,1)}, bf16[2,384,2048]{2,1,0:T(8,128)(2,1)S(1)}, bf16[2,512,768]{2,1,0:T(8,128)(2,1)S(1)}) custom-call(bf16[128,2048]{1,0:T(8,128)(2,1)S(1)} %copy-done.21, bf16[128,2048]{1,0:T(8,128)(2,1)S(1)} %collective-permute-done.56.refs_1_, bf16[128,2048]{1,0:T(8,128)(2,1)S(1)} %collective-permute-done.46.refs_2_, ...), custom_call_target="tpu_custom_call" | custom-call | flops 1073741824 | bytes 7432874 | tf_op jit(solution)/shard_map/cond/branch_1_fun/pallas_call | solution.py:93
  113.9 6.4 %branch_1_fun.28 = (bf16[2,768,768]{2,1,0:T(8,128)(2,1)S(1)}, bf16[2,2048,768]{2,1,0:T(8,128)(2,1)}) custom-call(bf16[2,2048,512]{2,1,0:T(8,128)(2,1)S(1)} %get-tuple-element.179.turned, bf16[2,512,768]{2,1,0:T(8,128)(2,1)S(1)} %get-tuple-element.187.grad_joint.left, bf16[2,2048,768]{2,1,0:T(8,128)(2,1)} %get-tuple-element.155.refs_9_.w, ...), custom_call_target="tpu_custom_call" | custom-call | flops 402653184 | bytes 9000277 | tf_op jit(solution)/shard_map/cond/branch_1_fun/pallas_call | solution.py:93
  121.3 8.1 %branch_1_fun.29 = (bf16[2,1024,768]{2,1,0:T(8,128)(2,1)S(1)}, bf16[2,2048,768]{2,1,0:T(8,128)(2,1)}) custom-call(bf16[2,2048,512]{2,1,0:T(8,128)(2,1)S(1)} %get-tuple-element.179.turned, bf16[2,512,768]{2,1,0:T(8,128)(2,1)S(1)} %get-tuple-element.187.grad_joint.left, ...), custom_call_target="tpu_custom_call", output_to_operand_aliasing={{1}: (4, {})} | custom-call | flops 536870912 | bytes 9262421 | tf_op jit(solution)/shard_map/cond/branch_1_fun/pallas_call | solution.py:93
  132.2 7.9 %branch_1_fun.31 = (f32[4,128,2048]{2,1,0:T(8,128)S(1)}, bf16[4,128,2048]{2,1,0:T(8,128)(2,1)}) custom-call(bf16[2,512,768]{2,1,0:T(8,128)(2,1)S(1)} %get-tuple-element.187.grad_joint.left, bf16[2,2048,768]{2,1,0:T(8,128)(2,1)} %get-tuple-element.155.refs_9_.w, f32[8,4,128]{2,1,0:T(4,128)S(1)} %gather_fusion.1), custom_call_target="tpu_custom_call" | custom-call | flops 1073741824 | bytes 4724053 | tf_op jit(solution)/shard_map/cond/branch_1_fun/pallas_call | solution.py:93
  140.1 7.1 %collective-permute-done.60.far.refs_6_ = bf16[128,2048]{1,0:T(8,128)(2,1)S(1)} collective-permute-done((bf16[128,2048]{1,0:T(8,128)(2,1)S(1)}, bf16[128,2048]{1,0:T(8,128)(2,1)S(1)}, u32[]{:S(2)}, u32[]{:S(2)}) %collective-permute-start.60) | collective-permute-done | bytes 524320 | tf_op jit(solution)/shard_map/cond/branch_1_fun/ppermute | solution.py:25
  153.0 21.4 %collective-permute-done.67.peer = bf16[2,768,768]{2,1,0:T(8,128)(2,1)S(1)} collective-permute-done((bf16[2,768,768]{2,1,0:T(8,128)(2,1)S(1)}, bf16[2,768,768]{2,1,0:T(8,128)(2,1)S(1)}, u32[]{:S(2)}, u32[]{:S(2)}) %collective-permute-start.67) | collective-permute-done | bytes 2359328 | tf_op jit(solution)/shard_map/cond/branch_1_fun/ppermute | solution.py:38
  179.2 6.8 %collective-permute-start.69 = (bf16[128,2048]{1,0:T(8,128)(2,1)S(1)}, bf16[128,2048]{1,0:T(8,128)(2,1)S(1)}, u32[]{:S(2)}, u32[]{:S(2)}) collective-permute-start(bf16[128,2048]{1,0:T(8,128)(2,1)S(1)} %get-tuple-element.207), channel_id=1, source_target_pairs={{0,2},{1,3},{2,6},{3,7},{4,0},{5,1},{6,4},{7,5},{8,10},{9,11},{10,... | collective-permute-start | bytes 1572872 | tf_op jit(solution)/shard_map/cond/branch_1_fun/ppermute | solution.py:33
  189.6 5.7 %branch_1_fun.36 = bf16[2,384,2048]{2,1,0:T(8,128)(2,1)} custom-call(bf16[128,2048]{1,0:T(8,128)(2,1)S(1)} %collective-permute-done.41.value.refs_0_, bf16[128,2048]{1,0:T(8,128)(2,1)S(1)} %collective-permute-done.71.refs_1_, bf16[128,2048]{1,0:T(8,128)(2,1)S(1)} %collective-permute-done.59.refs_2_, bf16[128,2048]{1,0:T(8,128)(2,1)S(1)} %collective-permute-done.72.refs_3_, ...), custom_call_target="tpu_custom_call" | custom-call | flops 536870912 | bytes 4811434 | tf_op jit(solution)/shard_map/cond/branch_1_fun/pallas_call | solution.py:93
  195.3 4.1 %collective-permute-done.69.middle.refs_0_ = bf16[128,2048]{1,0:T(8,128)(2,1)S(1)} collective-permute-done((bf16[128,2048]{1,0:T(8,128)(2,1)S(1)}, bf16[128,2048]{1,0:T(8,128)(2,1)S(1)}, u32[]{:S(2)}, u32[]{:S(2)}) %collective-permute-start.69) | collective-permute-done | bytes 524320 | tf_op jit(solution)/shard_map/cond/branch_1_fun/ppermute | solution.py:33
  199.4 11.1 %collective-permute-done.70.refs_1_ = bf16[128,2048]{1,0:T(8,128)(2,1)S(1)} collective-permute-done((bf16[128,2048]{1,0:T(8,128)(2,1)S(1)}, bf16[128,2048]{1,0:T(8,128)(2,1)S(1)}, u32[]{:S(2)}, u32[]{:S(2)}) %collective-permute-start.70) | collective-permute-done | bytes 524320 | tf_op jit(solution)/shard_map/cond/branch_1_fun/ppermute | solution.py:25
  212.2 14.6 %collective-permute-done.75.refs_2_ = bf16[128,2048]{1,0:T(8,128)(2,1)S(1)} collective-permute-done((bf16[128,2048]{1,0:T(8,128)(2,1)S(1)}, bf16[128,2048]{1,0:T(8,128)(2,1)S(1)}, u32[]{:S(2)}, u32[]{:S(2)}) %collective-permute-start.75) | collective-permute-done | bytes 524320 | tf_op jit(solution)/shard_map/cond/branch_1_fun/ppermute | solution.py:25
  228.4 13.4 %collective-permute-done.77.peer = bf16[2,1024,768]{2,1,0:T(8,128)(2,1)S(1)} collective-permute-done((bf16[2,1024,768]{2,1,0:T(8,128)(2,1)S(1)}, bf16[2,1024,768]{2,1,0:T(8,128)(2,1)S(1)}, u32[]{:S(2)}, u32[]{:S(2)}) %collective-permute-start.77) | collective-permute-done | bytes 3145760 | tf_op jit(solution)/shard_map/cond/branch_1_fun/ppermute | solution.py:38
  241.9 3.6 %branch_1_fun.40.rest_0_ = bf16[2,2048,768]{2,1,0:T(8,128)(2,1)} custom-call(bf16[2,1024,768]{2,1,0:T(8,128)(2,1)S(1)} %get-tuple-element.222.own, bf16[2,1024,768]{2,1,0:T(8,128)(2,1)S(1)} %collective-permute-done.77.peer, bf16[2,2048,768]{2,1,0:T(8,128)(2,1)} %branch_1_fun.34.rest_0_), custom_call_target="tpu_custom_call", output_to_operand_aliasing={{}: (2, {})} | custom-call | bytes 4194304 | tf_op jit(solution)/shard_map/cond/branch_1_fun/pallas_call | solution.py:93
  245.5 11.3 %collective-permute-done.76.peer = bf16[2,256,768]{2,1,0:T(8,128)(2,1)S(1)} collective-permute-done((bf16[2,256,768]{2,1,0:T(8,128)(2,1)}, bf16[2,256,768]{2,1,0:T(8,128)(2,1)S(1)}, u32[]{:S(2)}, u32[]{:S(2)}) %collective-permute-start.76) | collective-permute-done | bytes 786464 | tf_op jit(solution)/shard_map/cond/branch_1_fun/ppermute | solution.py:38
  (118 shorter events, 62.5 us)
Async XLA Ops:
  1.5 30.5 %collective-permute-start.39 = (bf16[128,2048]{1,0:T(8,128)(2,1)}, bf16[128,2048]{1,0:T(8,128)(2,1)S(1)}, u32[]{:S(2)}, u32[]{:S(2)}) collective-permute-start(bf16[128,2048]{1,0:T(8,128)(2,1)} %get-tuple-element.154.value.refs_0_.base), channel_id=1, source_target_pairs={{0,2},{1,3},{2,0},{3,1},{4,6},{5,7},{6,4},{7,5},{8,10},{9,11},{10,... | collective-permute-start | bytes 1572872 | tf_op jit(solution)/shard_map/cond/branch_1_fun/ppermute | solution.py:25
  4.6 27.5 %collective-permute-start.40 = (bf16[128,2048]{1,0:T(8,128)(2,1)}, bf16[128,2048]{1,0:T(8,128)(2,1)S(1)}, u32[]{:S(2)}, u32[]{:S(2)}) collective-permute-start(bf16[128,2048]{1,0:T(8,128)(2,1)} %get-tuple-element.154.value.refs_0_.base), channel_id=1, source_target_pairs={{0,6},{1,7},{2,4},{3,5},{4,2},{5,3},{6,0},{7,1},{8,14},{9,15},{10,... | collective-permute-start | bytes 1572872 | tf_op jit(solution)/shard_map/cond/branch_1_fun/ppermute | solution.py:25
  7.1 13.3 %collective-permute-start.41 = (bf16[128,2048]{1,0:T(8,128)(2,1)}, bf16[128,2048]{1,0:T(8,128)(2,1)S(1)}, u32[]{:S(2)}, u32[]{:S(2)}) collective-permute-start(bf16[128,2048]{1,0:T(8,128)(2,1)} %get-tuple-element.169.value.refs_0_.base), channel_id=1, source_target_pairs={{0,16},{8,24},{16,0},{24,8},{1,17},{9,25},{17,1},{25,9},{2,18},{10... | collective-permute-start | bytes 1572872 | tf_op jit(solution)/shard_map/cond/branch_1_fun/ppermute | solution.py:38
  20.4 12.4 %collective-permute-start.42 = (bf16[2,64,2048]{2,1,0:T(8,128)(2,1)}, bf16[2,64,2048]{2,1,0:T(8,128)(2,1)S(1)}, u32[]{:S(2)}, u32[]{:S(2)}) collective-permute-start(bf16[2,64,2048]{2,1,0:T(8,128)(2,1)} %get-tuple-element.140), channel_id=1, source_target_pairs={{0,16},{8,24},{16,0},{24,8},{1,17},{9,25},{17,1},{25,9},{2,18},{10... | collective-permute-start | bytes 1572872 | tf_op jit(solution)/shard_map/cond/branch_1_fun/ppermute | solution.py:38
  33.1 13.6 %collective-permute-start.44 = (bf16[2,64,2048]{2,1,0:T(8,128)(2,1)}, bf16[2,64,2048]{2,1,0:T(8,128)(2,1)S(1)}, u32[]{:S(2)}, u32[]{:S(2)}) collective-permute-start(bf16[2,64,2048]{2,1,0:T(8,128)(2,1)} %get-tuple-element.146), channel_id=1, source_target_pairs={{0,16},{8,24},{16,0},{24,8},{1,17},{9,25},{17,1},{25,9},{2,18},{10... | collective-permute-start | bytes 1572872 | tf_op jit(solution)/shard_map/cond/branch_1_fun/ppermute | solution.py:38
  34.7 12.8 %collective-permute-start.43 = (bf16[128,2048]{1,0:T(8,128)(2,1)S(1)}, bf16[128,2048]{1,0:T(8,128)(2,1)S(1)}, u32[]{:S(2)}, u32[]{:S(2)}) collective-permute-start(bf16[128,2048]{1,0:T(8,128)(2,1)S(1)} %branch_1_fun.22), channel_id=1, source_target_pairs={{0,4},{1,5},{2,0},{3,1},{4,6},{5,7},{6,2},{7,3},{8,12},{9,13},{10,... | collective-permute-start | bytes 1572872 | tf_op jit(solution)/shard_map/cond/branch_1_fun/ppermute | solution.py:33
  47.4 31.9 %collective-permute-start.52 = (bf16[2,176,2048]{2,1,0:T(8,128)(2,1)}, bf16[2,176,2048]{2,1,0:T(8,128)(2,1)S(1)}, u32[]{:S(2)}, u32[]{:S(2)}) collective-permute-start(bf16[2,176,2048]{2,1,0:T(8,128)(2,1)} %get-tuple-element.158), channel_id=1, source_target_pairs={{0,16},{8,24},{16,0},{24,8},{1,17},{9,25},{17,1},{25,9},{2,18},{10... | collective-permute-start | bytes 4325384 | tf_op jit(solution)/shard_map/cond/branch_1_fun/ppermute | solution.py:38
  50.4 18.6 %collective-permute-start.46 = (bf16[128,2048]{1,0:T(8,128)(2,1)S(1)}, bf16[128,2048]{1,0:T(8,128)(2,1)S(1)}, u32[]{:S(2)}, u32[]{:S(2)}) collective-permute-start(bf16[128,2048]{1,0:T(8,128)(2,1)S(1)} %copy-done.21), channel_id=1, source_target_pairs={{0,2},{1,3},{2,0},{3,1},{4,6},{5,7},{6,4},{7,5},{8,10},{9,11},{10,... | collective-permute-start | bytes 1572872 | tf_op jit(solution)/shard_map/cond/branch_1_fun/ppermute | solution.py:25
  51.3 25.5 %collective-permute-start.47 = (bf16[128,2048]{1,0:T(8,128)(2,1)S(1)}, bf16[128,2048]{1,0:T(8,128)(2,1)S(1)}, u32[]{:S(2)}, u32[]{:S(2)}) collective-permute-start(bf16[128,2048]{1,0:T(8,128)(2,1)S(1)} %copy-done.21), channel_id=1, source_target_pairs={{0,6},{1,7},{2,4},{3,5},{4,2},{5,3},{6,0},{7,1},{8,14},{9,15},{10,... | collective-permute-start | bytes 1572872 | tf_op jit(solution)/shard_map/cond/branch_1_fun/ppermute | solution.py:25
  79.7 17.1 %collective-permute-start.55 = (bf16[2,80,2048]{2,1,0:T(8,128)(2,1)S(1)}, bf16[2,80,2048]{2,1,0:T(8,128)(2,1)S(1)}, u32[]{:S(2)}, u32[]{:S(2)}) collective-permute-start(bf16[2,80,2048]{2,1,0:T(8,128)(2,1)S(1)} %copy-done.29), channel_id=1, source_target_pairs={{0,16},{8,24},{16,0},{24,8},{1,17},{9,25},{17,1},{25,9},{2,18},{10... | collective-permute-start | bytes 1966088 | tf_op jit(solution)/shard_map/cond/branch_1_fun/ppermute | solution.py:38
  80.5 14.3 %collective-permute-start.53 = (bf16[128,2048]{1,0:T(8,128)(2,1)S(1)}, bf16[128,2048]{1,0:T(8,128)(2,1)S(1)}, u32[]{:S(2)}, u32[]{:S(2)}) collective-permute-start(bf16[128,2048]{1,0:T(8,128)(2,1)S(1)} %branch_1_fun.25), channel_id=1, source_target_pairs={{0,4},{1,5},{2,0},{3,1},{4,6},{5,7},{6,2},{7,3},{8,12},{9,13},{10,... | collective-permute-start | bytes 1572872 | tf_op jit(solution)/shard_map/cond/branch_1_fun/ppermute | solution.py:33
  96.8 23.4 %collective-permute-start.62 = (bf16[2,384,512]{2,1,0:T(8,128)(2,1)S(1)}, bf16[2,384,512]{2,1,0:T(8,128)(2,1)S(1)}, u32[]{:S(2)}, u32[]{:S(2)}) collective-permute-start(bf16[2,384,512]{2,1,0:T(8,128)(2,1)S(1)} %get-tuple-element.183.refs_9_), channel_id=1, source_target_pairs={{0,16},{8,24},{16,0},{24,8},{1,17},{9,25},{17,1},{25,9},{2,18},{10... | collective-permute-start | bytes 2359304 | tf_op jit(solution)/shard_map/cond/branch_1_fun/ppermute | solution.py:38
  97.4 42.8 %collective-permute-start.63 = (bf16[128,2048]{1,0:T(8,128)(2,1)S(1)}, bf16[128,2048]{1,0:T(8,128)(2,1)S(1)}, u32[]{:S(2)}, u32[]{:S(2)}) collective-permute-start(bf16[128,2048]{1,0:T(8,128)(2,1)S(1)} %get-tuple-element.192), channel_id=1, source_target_pairs={{0,2},{1,3},{2,6},{3,7},{4,0},{5,1},{6,4},{7,5},{8,10},{9,11},{10,... | collective-permute-start | bytes 1572872 | tf_op jit(solution)/shard_map/cond/branch_1_fun/ppermute | solution.py:33
  98.4 41.7 %collective-permute-start.64 = (bf16[128,2048]{1,0:T(8,128)(2,1)S(1)}, bf16[128,2048]{1,0:T(8,128)(2,1)S(1)}, u32[]{:S(2)}, u32[]{:S(2)}) collective-permute-start(bf16[128,2048]{1,0:T(8,128)(2,1)S(1)} %get-tuple-element.193), channel_id=1, source_target_pairs={{0,2},{1,3},{2,0},{3,1},{4,6},{5,7},{6,4},{7,5},{8,10},{9,11},{10,... | collective-permute-start | bytes 1572872 | tf_op jit(solution)/shard_map/cond/branch_1_fun/ppermute | solution.py:25
  101.2 38.9 %collective-permute-start.59 = (bf16[128,2048]{1,0:T(8,128)(2,1)S(1)}, bf16[128,2048]{1,0:T(8,128)(2,1)S(1)}, u32[]{:S(2)}, u32[]{:S(2)}) collective-permute-start(bf16[128,2048]{1,0:T(8,128)(2,1)S(1)} %collective-permute-done.41.value.refs_0_), channel_id=1, source_target_pairs={{0,2},{1,3},{2,0},{3,1},{4,6},{5,7},{6,4},{7,5},{8,10},{9,11},{10,... | collective-permute-start | bytes 1572872 | tf_op jit(solution)/shard_map/cond/branch_1_fun/ppermute | solution.py:25
  101.3 46.0 %collective-permute-start.60 = (bf16[128,2048]{1,0:T(8,128)(2,1)S(1)}, bf16[128,2048]{1,0:T(8,128)(2,1)S(1)}, u32[]{:S(2)}, u32[]{:S(2)}) collective-permute-start(bf16[128,2048]{1,0:T(8,128)(2,1)S(1)} %collective-permute-done.41.value.refs_0_), channel_id=1, source_target_pairs={{0,6},{1,7},{2,4},{3,5},{4,2},{5,3},{6,0},{7,1},{8,14},{9,15},{10,... | collective-permute-start | bytes 1572872 | tf_op jit(solution)/shard_map/cond/branch_1_fun/ppermute | solution.py:25
  120.3 54.2 %collective-permute-start.67 = (bf16[2,768,768]{2,1,0:T(8,128)(2,1)S(1)}, bf16[2,768,768]{2,1,0:T(8,128)(2,1)S(1)}, u32[]{:S(2)}, u32[]{:S(2)}) collective-permute-start(bf16[2,768,768]{2,1,0:T(8,128)(2,1)S(1)} %get-tuple-element.202.own), channel_id=1, source_target_pairs={{0,16},{8,24},{16,0},{24,8},{1,17},{9,25},{17,1},{25,9},{2,18},{10... | collective-permute-start | bytes 7077896 | tf_op jit(solution)/shard_map/cond/branch_1_fun/ppermute | solution.py:38
  147.6 94.3 %collective-permute-start.77 = (bf16[2,1024,768]{2,1,0:T(8,128)(2,1)S(1)}, bf16[2,1024,768]{2,1,0:T(8,128)(2,1)S(1)}, u32[]{:S(2)}, u32[]{:S(2)}) collective-permute-start(bf16[2,1024,768]{2,1,0:T(8,128)(2,1)S(1)} %get-tuple-element.222.own), channel_id=1, source_target_pairs={{0,16},{8,24},{16,0},{24,8},{1,17},{9,25},{17,1},{25,9},{2,18},{10... | collective-permute-start | bytes 9437192 | tf_op jit(solution)/shard_map/cond/branch_1_fun/ppermute | solution.py:38
  149.0 28.2 %collective-permute-start.68 = (bf16[128,2048]{1,0:T(8,128)(2,1)S(1)}, bf16[128,2048]{1,0:T(8,128)(2,1)S(1)}, u32[]{:S(2)}, u32[]{:S(2)}) collective-permute-start(bf16[128,2048]{1,0:T(8,128)(2,1)S(1)} %branch_1_fun.35), channel_id=1, source_target_pairs={{0,6},{1,7},{2,4},{3,5},{4,2},{5,3},{6,0},{7,1},{8,14},{9,15},{10,... | collective-permute-start | bytes 1572872 | tf_op jit(solution)/shard_map/cond/branch_1_fun/ppermute | solution.py:25
  150.7 26.5 %collective-permute-start.66 = (bf16[128,2048]{1,0:T(8,128)(2,1)S(1)}, bf16[128,2048]{1,0:T(8,128)(2,1)S(1)}, u32[]{:S(2)}, u32[]{:S(2)}) collective-permute-start(bf16[128,2048]{1,0:T(8,128)(2,1)S(1)} %branch_1_fun.32), channel_id=1, source_target_pairs={{0,4},{1,5},{2,0},{3,1},{4,6},{5,7},{6,2},{7,3},{8,12},{9,13},{10,... | collective-permute-start | bytes 1572872 | tf_op jit(solution)/shard_map/cond/branch_1_fun/ppermute | solution.py:33
  179.2 20.3 %collective-permute-start.69 = (bf16[128,2048]{1,0:T(8,128)(2,1)S(1)}, bf16[128,2048]{1,0:T(8,128)(2,1)S(1)}, u32[]{:S(2)}, u32[]{:S(2)}) collective-permute-start(bf16[128,2048]{1,0:T(8,128)(2,1)S(1)} %get-tuple-element.207), channel_id=1, source_target_pairs={{0,2},{1,3},{2,6},{3,7},{4,0},{5,1},{6,4},{7,5},{8,10},{9,11},{10,... | collective-permute-start | bytes 1572872 | tf_op jit(solution)/shard_map/cond/branch_1_fun/ppermute | solution.py:33
  185.9 24.6 %collective-permute-start.70 = (bf16[128,2048]{1,0:T(8,128)(2,1)S(1)}, bf16[128,2048]{1,0:T(8,128)(2,1)S(1)}, u32[]{:S(2)}, u32[]{:S(2)}) collective-permute-start(bf16[128,2048]{1,0:T(8,128)(2,1)S(1)} %get-tuple-element.208), channel_id=1, source_target_pairs={{0,2},{1,3},{2,0},{3,1},{4,6},{5,7},{6,4},{7,5},{8,10},{9,11},{10,... | collective-permute-start | bytes 1572872 | tf_op jit(solution)/shard_map/cond/branch_1_fun/ppermute | solution.py:25
  186.7 70.1 %collective-permute-start.76 = (bf16[2,256,768]{2,1,0:T(8,128)(2,1)}, bf16[2,256,768]{2,1,0:T(8,128)(2,1)S(1)}, u32[]{:S(2)}, u32[]{:S(2)}) collective-permute-start(bf16[2,256,768]{2,1,0:T(8,128)(2,1)} %get-tuple-element.186.own), channel_id=1, source_target_pairs={{0,16},{8,24},{16,0},{24,8},{1,17},{9,25},{17,1},{25,9},{2,18},{10... | collective-permute-start | bytes 2359304 | tf_op jit(solution)/shard_map/cond/branch_1_fun/ppermute | solution.py:38
  210.9 15.8 %collective-permute-start.75 = (bf16[128,2048]{1,0:T(8,128)(2,1)S(1)}, bf16[128,2048]{1,0:T(8,128)(2,1)S(1)}, u32[]{:S(2)}, u32[]{:S(2)}) collective-permute-start(bf16[128,2048]{1,0:T(8,128)(2,1)S(1)} %branch_1_fun.38), channel_id=1, source_target_pairs={{0,6},{1,7},{2,4},{3,5},{4,2},{5,3},{6,0},{7,1},{8,14},{9,15},{10,... | collective-permute-start | bytes 1572872 | tf_op jit(solution)/shard_map/cond/branch_1_fun/ppermute | solution.py:25
  (31 other events, 313.7 us)

commit v2 on v1

--- a/solution.py
+++ b/solution.py
@@ -14,7 +14,8 @@
 COLS = 512
 DEEP = 256
 SCALARS = ()
-PIECES = (4, 4, 11, 5)
+PIECES = (4, 4, 10, 4)
+LAST_PIECE = 2
 F32 = jnp.float32
 BF16 = jnp.bfloat16
 VMEM = 32 * 1024 * 1024
@@ -99,7 +100,7 @@
         scratch_shapes=list(scratch),
         input_output_aliases=aliases or {},
         compiler_params=pltpu.CompilerParams(vmem_limit_bytes=VMEM),
-        cost_estimate=pl.CostEstimate(flops=flops // 3, bytes_accessed=moved // 3, transcendentals=0),
+        cost_estimate=pl.CostEstimate(flops=flops, bytes_accessed=moved, transcendentals=0),
     )(*[a for a, _, _ in ins])
 
 
@@ -113,32 +114,40 @@
     return [mine_ref[k, 2 * a : 2 * a + 1, :] == slot for a in range(local)]
 
 
-def onehot(found):
-    return jnp.concatenate([f.astype(F32) for f in found], axis=0).astype(BF16)
-
-
-def row_weights(mine_ref, k, found):
-    return [
-        jnp.sum(jnp.where(f, mine_ref[k, 2 * a + 1 : 2 * a + 2, :], 0.0), axis=1, keepdims=True)
-        for a, f in enumerate(found)
-    ]
-
-
-def fill_rows(blocks, mine_ref, rows_ref, local, weighted):
+def kept_routing(groups, local, tokens, weighted):
+    hot = pltpu.VMEM((groups, local * CAP, tokens), BF16)
+    return [hot, pltpu.VMEM((groups, local * CAP, 1), F32)] if weighted else [hot]
+
+
+def find_rows(mine_ref, local, hot, weight=None):
+    @pl.when(pl.program_id(0) == 0)
+    def _():
+        for k in range(hot.shape[0]):
+            found = matches(mine_ref, k, local)
+            hot[k] = jnp.concatenate([f.astype(F32) for f in found], axis=0).astype(BF16)
+            if weight is not None:
+                one = [
+                    jnp.sum(jnp.where(f, mine_ref[k, 2 * a + 1 : 2 * a + 2, :], 0.0), axis=1, keepdims=True)
+                    for a, f in enumerate(found)
+                ]
+                weight[k] = jnp.concatenate(one, axis=0)
+
+
+def fill_rows(blocks, mine_ref, rows_ref, local, hot, weight=None):
+    find_rows(mine_ref, local, hot, weight)
     for k, block in enumerate(blocks):
-        found = matches(mine_ref, k, local)
-        rows = nn(onehot(found), block[...])
-        weight = row_weights(mine_ref, k, found) if weighted else None
+        rows = nn(hot[k], block[...])
+        if weight is not None:
+            rows = rows * weight[k]
         for a in range(local):
-            part = rows[a * CAP : (a + 1) * CAP]
-            if weighted:
-                part = part * weight[a]
-            rows_ref[a, k * CAP : (k + 1) * CAP, :] = part.astype(BF16)
+            rows_ref[a, k * CAP : (k + 1) * CAP, :] = rows[a * CAP : (a + 1) * CAP].astype(BF16)
 
 
 def forward_body(groups, local, hidden, scale, *refs):
-    blocks, (mine, w, turned, inner, turned_inner, slope, value, joint, rows) = refs[:groups], refs[groups:]
-    fill_rows(blocks, mine, rows, local, False)
+    blocks, (mine, w, last_w, last_mom, turned, inner, packet, slope, value, joint, rows, hot) = refs[:groups], refs[groups:]
+    base = (last_w[...].astype(F32) - (STEP_SIZE * MOMENTUM_DECAY) * last_mom[...].astype(F32)).astype(BF16)
+    packet[:, last_rows(hidden, base.shape[1]), : base.shape[2]] = base
+    fill_rows(blocks, mine, rows, local, hot)
     first = pl.program_id(0) == 0
 
     for a in range(local):
@@ -161,37 +170,45 @@
             sigmoid = jax.nn.sigmoid(gate)
             act = gate * sigmoid
             inner[a] = (act * upper).astype(BF16)
-            turned_inner[a] = inner[a].T
+            packet[a, :hidden] = inner[a].T
             slope[a] = upper * (sigmoid * (1.0 + gate * (1.0 - sigmoid)))
             value[a] = act
 
 
-def forward(blocks, mine, proj_in):
+def last_rows(hidden, size):
+    return pl.ds(pl.multiple_of(hidden + pl.program_id(0) * size, size), size)
+
+
+def forward(blocks, mine, proj_in, proj_out, mom_out):
     groups = len(blocks)
     local, width, double = proj_in.shape
     hidden, rows, tokens = double // 2, groups * CAP, blocks[0].shape[0]
+    last = hidden // 24 * LAST_PIECE
+    tall = hidden + last * (width // COLS)
     whole = lambda j: (0, 0, 0)
     return kernel_call(
         partial(forward_body, groups, local, hidden, 1.0 / math.sqrt(width)),
         (width // COLS,),
         [(b, (tokens, COLS), lambda j: (0, j)) for b in blocks]
-        + [(mine, mine.shape, whole), (proj_in, (local, COLS, double), lambda j: (0, j, 0))],
+        + [(mine, mine.shape, whole), (proj_in, (local, COLS, double), lambda j: (0, j, 0))]
+        + [(v, (local, last, COLS), lambda j: (0, hidden // last - 1, j)) for v in (proj_out, mom_out)],
         [
             (shape((local, width, rows), BF16), (local, COLS, rows), lambda j: (0, j, 0)),
             (shape((local, rows, hidden), BF16), (local, rows, hidden), whole),
-            (shape((local, hidden, rows), BF16), (local, hidden, rows), whole),
+            (shape((local, tall, rows), BF16), (local, tall, rows), whole),
             (shape((local, rows, hidden), F32), (local, rows, hidden), whole),
             (shape((local, rows, hidden), F32), (local, rows, hidden), whole),
         ],
-        [pltpu.VMEM((local, rows, double), F32), pltpu.VMEM((local, rows, COLS), BF16)],
+        [pltpu.VMEM((local, rows, double), F32), pltpu.VMEM((local, rows, COLS), BF16)]
+        + kept_routing(groups, local, tokens, False),
         2 * local * rows * width * double,
     )
 
 
 def backward_body(groups, local, hidden, scale, *refs):
     blocks = refs[:groups]
-    mine, turned_inner, slope, value, w, mom, new_mom, update, grad_joint, rows, grad_inner = refs[groups:]
-    fill_rows(blocks, mine, rows, local, True)
+    mine, turned_inner, slope, value, w, mom, new_mom, update, grad_joint, rows, grad_inner, hot, weight = refs[groups:]
+    fill_rows(blocks, mine, rows, local, hot, weight)
     first = pl.program_id(0) == 0
 
     for a in range(local):
@@ -233,22 +250,26 @@
             (proj_out, *cut),
             (shape((local, rows, 2 * hidden), BF16), (local, rows, 2 * hidden), whole),
         ],
-        [pltpu.VMEM((local, rows, COLS), BF16), pltpu.VMEM((local, rows, hidden), F32)],
+        [pltpu.VMEM((local, rows, COLS), BF16), pltpu.VMEM((local, rows, hidden), F32)]
+        + kept_routing(groups, local, tokens, True),
         4 * local * rows * width * hidden,
         kept=(0,),
     )
 
 
 def peer_body(groups, local, scale, *refs):
-    blocks, (mine, turned_inner, *bases, update, new_w, rows) = refs[:groups], refs[groups:]
-    fill_rows(blocks, mine, rows, local, True)
+    blocks, (mine, packet, *bases, update, new_w, rows, hot, weight) = refs[:groups], refs[groups:]
+    hidden, width = update.shape[1:]
+    last = hidden - sum(base.shape[1] for base in bases)
+    fill_rows(blocks, mine, rows, local, hot, weight)
     for a in range(local):
-        whole = jnp.concatenate([base[a].astype(F32) for base in bases], axis=0)
-        theirs = whole - STEP_SIZE * (nn(turned_inner[a], rows[a]) * scale)
+        below = packet[a, last_rows(hidden, last), :width]
+        whole = jnp.concatenate([base[a].astype(F32) for base in bases] + [below.astype(F32)], axis=0)
+        theirs = whole - STEP_SIZE * (nn(packet[a, :hidden], rows[a]) * scale)
         new_w[a] = (0.5 * (update[a].astype(F32) + theirs)).astype(BF16)
 
 
-def peer_out(blocks, mine, turned_inner, bases, update):
+def peer_out(blocks, mine, packet, bases, update):
     groups = len(blocks)
     local, hidden, width = update.shape
     rows, tokens = groups * CAP, blocks[0].shape[0]
@@ -258,11 +279,11 @@
         partial(peer_body, groups, local, 1.0 / math.sqrt(hidden)),
         (width // COLS,),
         [(b, (tokens, COLS), lambda j: (0, j)) for b in blocks]
-        + [(mine, mine.shape, whole), (turned_inner, (local, hidden, rows), whole)]
+        + [(mine, mine.shape, whole), (packet, packet.shape, whole)]
         + [(b, (local, b.shape[1], COLS), lambda j: (0, 0, j)) for b in bases]
         + [(update, *cut)],
         [(update, *cut)],
-        [pltpu.VMEM((local, rows, COLS), BF16)],
+        [pltpu.VMEM((local, rows, COLS), BF16)] + kept_routing(groups, local, tokens, True),
         2 * local * rows * width * hidden,
         kept=(0,),
     )[0]
@@ -336,16 +357,15 @@
     )[0]
 
 
-def returns_body(groups, local, scale, weighted, product, left, w, mine, own, other, rows):
+def returns_body(groups, local, scale, product, left, w, mine, own, other, rows, hot, weight=None):
+    find_rows(mine, local, hot, weight)
     for a in range(local):
         rows[a] = (product(left[a], w[a]) * scale).astype(rows.dtype)
     for k in range(groups):
-        found = matches(mine, k, local)
-        weight = row_weights(mine, k, found) if weighted else None
-        parts = [rows[a, k * CAP : (k + 1) * CAP, :] for a in range(local)]
-        if weighted:
-            parts = [p * weight[a] for a, p in enumerate(parts)]
-        part = tn(onehot(found), jnp.concatenate([p.astype(BF16) for p in parts], axis=0))
+        parts = jnp.concatenate([rows[a, k * CAP : (k + 1) * CAP, :] for a in range(local)], axis=0)
+        if weight is not None:
+            parts = parts * weight[k]
+        part = tn(hot[k], parts.astype(BF16))
         if k % 2 == 0:
             own[k // 2] = part
         else:
@@ -362,11 +382,11 @@
         product, width, cut, scale = nt, w.shape[1], ((local, COLS, inside), lambda j: (0, j, 0)), 1.0 / math.sqrt(w.shape[1])
     out = ((groups // 2, tokens, COLS), lambda j: (0, 0, j))
     return kernel_call(
-        partial(returns_body, groups, local, scale, weighted, product),
+        partial(returns_body, groups, local, scale, product),
         (width // COLS,),
         [(left, left.shape, whole), (w, *cut), (mine, mine.shape, whole)],
         [(shape((groups // 2, tokens, width), F32), *out), (shape((groups // 2, tokens, width), BF16), *out)],
-        [pltpu.VMEM((local, rows, COLS), F32 if weighted else BF16)],
+        [pltpu.VMEM((local, rows, COLS), F32 if weighted else BF16)] + kept_routing(groups, local, tokens, weighted),
         2 * local * rows * width * inside,
     )
 
@@ -465,7 +485,7 @@
     upstream_now, base = ties((upstream, bases[2], *tok_same[1:], peer_bases[1]))[:2]
     cot = near_and_far(upstream_now)
     peer_bases.append(gossip(base, bit))
-    turned_rows, inner, turned_inner, slope, value = forward(with_other_core(tok_same), mine, proj_in)
+    turned_rows, inner, packet, slope, value = forward(with_other_core(tok_same), mine, proj_in, proj_out, mom_out)
     own, other = returns(inner, proj_out, mine, True)
     *cot, own, peer_bases[2] = ties((*cot, own, peer_bases[2]))
     sent = middle_of(upstream, cot, ends)
@@ -476,12 +496,12 @@
     early = [0, 1, 3] if len(cot_same) == 4 else []
     swapped = {s: swap(cot_same[s]) for s in early}
     *cot_same, total_1, peer_bases[3], swapped = ties((*cot_same, total_1, peer_bases[3], swapped))
-    peer_inner = gossip(after(turned_inner, peer_bases[3]), bit)
+    peer_packet = gossip(after(packet, peer_bases[3]), bit)
     cot_all = [part for s, block in enumerate(cot_same) for part in (block, swapped[s] if s in swapped else swap(block))]
-    new_mom_out, update_out, grad_joint = backward(cot_all, mine, turned_inner, slope, value, proj_out, mom_out)
+    new_mom_out, update_out, grad_joint = backward(cot_all, mine, packet, slope, value, proj_out, mom_out)
     update_0, new_mom_in = grad_in(turned_rows, grad_joint, proj_in, mom_in, 0, first_rows, None)
     peer_0 = gossip(update_0, bit)
-    new_mom_in, peer_inner = ties((new_mom_in, peer_inner))
+    new_mom_in, peer_packet = ties((new_mom_in, peer_packet))
     heard_1 = send_first(parts_1, cot_same[2])
     there = near_and_far(after(peer_upstream, cot_same[2]))
     last = width - DEEP
@@ -502,7 +522,7 @@
     layer_out = added(total_1, heard_1, ends)
     heard_2 = send_first(parts_2, there_same[2])
     there_all = with_other_core(there_same)
-    new_w_out = peer_out(there_all, peer_mine, peer_inner, peer_bases, update_out)
+    new_w_out = peer_out(there_all, peer_mine, peer_packet, peer_bases, update_out)
     *heard_2, new_w_out, layer_out = ties((*heard_2, new_w_out, layer_out))
     grad_tokens = added(total_2, send_last(parts_2, heard_2, ends), ends)
 

time: 259 us -> 255 us (0.985)
  waiting for transfers between devices: 131 us -> 123 us
  local copies, waits for them, and re-layouts: 3.01 us -> 6.94 us
    ppermute x5, waiting for transfers between devices: 12.9 us -> 1.75 us  [along_chips(): lax.ppermute(value, 'exp', [(2 * c + k, 2 * t + k) for c, t in enumerate(...]
    ppermute x10, waiting for transfers between devices: 68.2 us -> 74.4 us  [gossip(): return lax.ppermute(value, 'rep', [(i, i ^ 1 << bit) for i in range(size)])]
    cond x30 -> x52, local copies, waits for them, and re-layouts: 1.82 us -> 5.75 us
  transfers between devices with their start and end apart: 40 -> 40, of which waited for: 19 -> 18; matrix products, arithmetic and copies ran while one was open for 1% -> 1% of each run, Pallas kernels for 29% -> 29%
where the time goes in v2:
time: 255 us
  waiting for transfers between devices  123 us (48%)
  Pallas kernels  77.3 us (30%)
  starting transfers between devices  44.4 us (17%)
  local copies, waits for them, and re-layouts  6.94 us (3%)
    pallas_call x21, Pallas kernels, kernel_call(): pl.pallas_call(body, grid=grid, in_specs=[spec(b, w) for _, b, w in ins],...  77.3 us
    ppermute x10, waiting for transfers between devices, gossip(): return lax.ppermute(value, 'rep', [(i, i ^ 1 << bit) for i in range(size)])  74.4 us
    ppermute x24, waiting for transfers between devices, to_xor(): return lax.ppermute(value, 'exp', [(i, i ^ k) for i in range(size)])  41.7 us
    ppermute x24, starting transfers between devices, to_xor(): return lax.ppermute(value, 'exp', [(i, i ^ k) for i in range(size)])  19.4 us
    ppermute x10, starting transfers between devices, gossip(): return lax.ppermute(value, 'rep', [(i, i ^ 1 << bit) for i in range(size)])  11.4 us
    ppermute x5, starting transfers between devices, along_chips(): lax.ppermute(value, 'exp', [(2 * c + k, 2 * t + k) for c, t in enumerate(...  10.3 us
    cond x52, local copies, waits for them, and re-layouts  5.75 us
    all_to_all x1, waiting for transfers between devices, routing(): lax.all_to_all(packed, 'exp', split_axis=0, concat_axis=0, tiled=True)  5.54 us
  transfers between devices with their start and end apart: 40, of which 18 were waited for; matrix products, arithmetic and copies ran while one was open for 1% of the time, Pallas kernels for 29%

profile of v2, /device:TPU:0, one launch (start us, length us, event | category | flops | bytes accessed | tf_op | source)
XLA Modules:
  0.0 254.8 jit_solution(292341098290920351)
XLA Ops:
  1.3 253.5 %conditional.1 = (bf16[1,128,2048]{2,1,0:T(8,128)(2,1)}, bf16[1,128,2048]{2,1,0:T(8,128)(2,1)}, bf16[1,2,2048,768]{3,2,1,0:T(8,128)(2,1)}, bf16[1,2,384,2048]{3,...) conditional(s32[]{:T(128)} %clamp.3, (bf16[128,2048]{1,0:T(8,128)(2,1)}, ...), branch_computations={%region_0.3_spmd, %region_3.6_spmd} | conditional | flops 16106265600 | bytes 427185728 | solution.py:538
  1.5 3.1 %collective-permute-start.39 = (bf16[128,2048]{1,0:T(8,128)(2,1)}, bf16[128,2048]{1,0:T(8,128)(2,1)S(1)}, u32[]{:S(2)}, u32[]{:S(2)}) collective-permute-start(bf16[128,2048]{1,0:T(8,128)(2,1)} %get-tuple-element.154.value.refs_0_.base), channel_id=1, source_target_pairs={{0,2},{1,3},{2,0},{3,1},{4,6},{5,7},{6,4},{7,5},{8,10},{9,11},{10,... | collective-permute-start | bytes 1572872 | tf_op jit(solution)/shard_map/cond/branch_1_fun/ppermute | solution.py:26
  9.3 5.0 %branch_1_fun.21 = (bf16[2,64,2048]{2,1,0:T(8,128)(2,1)}, bf16[2,64,2048]{2,1,0:T(8,128)(2,1)}, bf16[2,160,2048]{2,1,0:T(8,128)(2,1)}, bf16[2,64,2048]{2,1,0:T(8,128)(2,1)}) custom-call(bf16[2,384,2048]{2,1,0:T(8,128)(2,1)} %get-tuple-element.137.w.refs_10_.refs_12_, bf16[2,384,2048]{2,1,0:T(8,128)(2,1)} %get-tuple-element.138.mom.refs_11_.refs_13_), custom_call_target="tpu_custom_call" | custom-call | bytes 9175040 | tf_op jit(solution)/shard_map/cond/branch_1_fun/pallas_call | solution.py:94
  14.4 6.0 %collective-permute-done.41.value.refs_0_ = bf16[128,2048]{1,0:T(8,128)(2,1)S(1)} collective-permute-done((bf16[128,2048]{1,0:T(8,128)(2,1)}, bf16[128,2048]{1,0:T(8,128)(2,1)S(1)}, u32[]{:S(2)}, u32[]{:S(2)}) %collective-permute-start.41) | collective-permute-done | bytes 524320 | tf_op jit(solution)/shard_map/cond/branch_1_fun/ppermute | solution.py:39
  22.6 3.3 %all-to-all-start.1 = ((f32[8,4,128]{2,1,0:T(4,128)}), f32[8,4,128]{2,1,0:T(4,128)S(1)}, u32[]{:S(2)}, u32[]{:S(2)}) async-start(f32[8,4,128]{2,1,0:T(4,128)} %bitcast.21), calls=%async_computation.1 | async-start | bytes 32768 | tf_op jit(solution)/shard_map/cond/branch_1_fun/all_to_all | solution.py:461
  26.0 5.5 %all-to-all-done.1 = f32[8,4,128]{2,1,0:T(4,128)S(1)} async-done(((f32[8,4,128]{2,1,0:T(4,128)}), f32[8,4,128]{2,1,0:T(4,128)S(1)}, u32[]{:S(2)}, u32[]{:S(2)}) %all-to-all-start.1) | async-done | bytes 16416 | tf_op jit(solution)/shard_map/cond/branch_1_fun/all_to_all | solution.py:461
  35.9 10.8 %collective-permute-done.45.refs_8_ = f32[8,4,128]{2,1,0:T(4,128)S(1)} collective-permute-done((f32[8,4,128]{2,1,0:T(4,128)S(1)}, f32[8,4,128]{2,1,0:T(4,128)S(1)}, u32[]{:S(2)}, u32[]{:S(2)}) %collective-permute-start.45) | collective-permute-done | bytes 16416 | tf_op jit(solution)/shard_map/cond/branch_1_fun/ppermute | solution.py:39
  53.5 11.0 %branch_1_fun.23 = (bf16[2,2048,512]{2,1,0:T(8,128)(2,1)S(1)}, bf16[2,512,384]{2,1,0:T(8,128)(2,1)S(1)}, bf16[2,512,512]{2,1,0:T(8,128)(2,1)S(1)}, f32[2,512,384]{2,1,0:T(8,128)S(1)}, f32[2,512,384]{2,1,0:T(8,128)S(1)}) custom-call(bf16[128,2048]{1,0:T(8,128)(2,1)S(1)} %copy-done.41, bf16[128,2048]{1,0:T(8,128)(2,1)S(1)} %collective-permute-done.48.refs_1_, ...), custom_call_target="tpu_custom_call" | custom-call | flops 3221225472 | bytes 25968640 | tf_op jit(solution)/shard_map/cond/branch_1_fun/pallas_call | solution.py:94
  64.6 4.8 %branch_1_fun.24 = (f32[4,128,2048]{2,1,0:T(8,128)S(1)}, bf16[4,128,2048]{2,1,0:T(8,128)(2,1)S(1)}) custom-call(bf16[2,512,384]{2,1,0:T(8,128)(2,1)S(1)} %get-tuple-element.156.left, bf16[2,384,2048]{2,1,0:T(8,128)(2,1)S(1)} %copy-done.39, f32[8,4,128]{2,1,0:T(4,128)S(1)} %gather_fusion.1), custom_call_target="tpu_custom_call" | custom-call | flops 1610612736 | bytes 10240000 | tf_op jit(solution)/shard_map/cond/branch_1_fun/pallas_call | solution.py:94
  69.4 7.4 %collective-permute-done.47.far.refs_6_ = bf16[128,2048]{1,0:T(8,128)(2,1)S(1)} collective-permute-done((bf16[128,2048]{1,0:T(8,128)(2,1)S(1)}, bf16[128,2048]{1,0:T(8,128)(2,1)S(1)}, u32[]{:S(2)}, u32[]{:S(2)}) %collective-permute-start.47) | collective-permute-done | bytes 524320 | tf_op jit(solution)/shard_map/cond/branch_1_fun/ppermute | solution.py:26
  83.3 9.8 %collective-permute-done.55.refs_13_ = bf16[2,64,2048]{2,1,0:T(8,128)(2,1)S(1)} collective-permute-done((bf16[2,64,2048]{2,1,0:T(8,128)(2,1)S(1)}, bf16[2,64,2048]{2,1,0:T(8,128)(2,1)S(1)}, u32[]{:S(2)}, u32[]{:S(2)}) %collective-permute-start.55) | collective-permute-done | bytes 524320 | tf_op jit(solution)/shard_map/cond/branch_1_fun/ppermute | solution.py:39
  98.9 10.6 %branch_1_fun.27 = (bf16[2,384,2048]{2,1,0:T(8,128)(2,1)}, bf16[2,384,2048]{2,1,0:T(8,128)(2,1)S(1)}, bf16[2,512,768]{2,1,0:T(8,128)(2,1)S(1)}) custom-call(bf16[128,2048]{1,0:T(8,128)(2,1)S(1)} %copy-done.43, bf16[128,2048]{1,0:T(8,128)(2,1)S(1)} %collective-permute-done.56.refs_1_, bf16[128,2048]{1,0:T(8,128)(2,1)S(1)} %collective-permute-done.46.refs_2_, ...), custom_call_target="tpu_custom_call" | custom-call | flops 3221225472 | bytes 22560768 | tf_op jit(solution)/shard_map/cond/branch_1_fun/pallas_call | solution.py:94
  109.6 6.3 %branch_1_fun.28 = (bf16[2,768,768]{2,1,0:T(8,128)(2,1)S(1)}, bf16[2,2048,768]{2,1,0:T(8,128)(2,1)}) custom-call(bf16[2,2048,512]{2,1,0:T(8,128)(2,1)S(1)} %get-tuple-element.179.turned, bf16[2,512,768]{2,1,0:T(8,128)(2,1)S(1)} %get-tuple-element.187.grad_joint.left, bf16[2,2048,768]{2,1,0:T(8,128)(2,1)} %get-tuple-element.155.refs_9_.w, ...), custom_call_target="tpu_custom_call" | custom-call | flops 1207959552 | bytes 27000832 | tf_op jit(solution)/shard_map/cond/branch_1_fun/pallas_call | solution.py:94
  118.2 8.1 %branch_1_fun.29 = (bf16[2,1024,768]{2,1,0:T(8,128)(2,1)S(1)}, bf16[2,2048,768]{2,1,0:T(8,128)(2,1)}) custom-call(bf16[2,2048,512]{2,1,0:T(8,128)(2,1)S(1)} %get-tuple-element.179.turned, bf16[2,512,768]{2,1,0:T(8,128)(2,1)S(1)} %get-tuple-element.187.grad_joint.left, ...), custom_call_target="tpu_custom_call", output_to_operand_aliasing={{1}: (4, {})} | custom-call | flops 1610612736 | bytes 27787264 | tf_op jit(solution)/shard_map/cond/branch_1_fun/pallas_call | solution.py:94
  129.2 7.1 %branch_1_fun.31 = (f32[4,128,2048]{2,1,0:T(8,128)S(1)}, bf16[4,128,2048]{2,1,0:T(8,128)(2,1)S(1)}) custom-call(bf16[2,512,768]{2,1,0:T(8,128)(2,1)S(1)} %get-tuple-element.187.grad_joint.left, bf16[2,2048,768]{2,1,0:T(8,128)(2,1)} %get-tuple-element.155.refs_9_.w, f32[8,4,128]{2,1,0:T(4,128)S(1)} %gather_fusion.1), custom_call_target="tpu_custom_call" | custom-call | flops 3221225472 | bytes 14172160 | tf_op jit(solution)/shard_map/cond/branch_1_fun/pallas_call | solution.py:94
  136.3 6.0 %collective-permute-done.64.refs_1_ = bf16[128,2048]{1,0:T(8,128)(2,1)S(1)} collective-permute-done((bf16[128,2048]{1,0:T(8,128)(2,1)S(1)}, bf16[128,2048]{1,0:T(8,128)(2,1)S(1)}, u32[]{:S(2)}, u32[]{:S(2)}) %collective-permute-start.64) | collective-permute-done | bytes 524320 | tf_op jit(solution)/shard_map/cond/branch_1_fun/ppermute | solution.py:26
  148.8 22.6 %collective-permute-done.67.peer = bf16[2,768,768]{2,1,0:T(8,128)(2,1)S(1)} collective-permute-done((bf16[2,768,768]{2,1,0:T(8,128)(2,1)S(1)}, bf16[2,768,768]{2,1,0:T(8,128)(2,1)S(1)}, u32[]{:S(2)}, u32[]{:S(2)}) %collective-permute-start.67) | collective-permute-done | bytes 2359328 | tf_op jit(solution)/shard_map/cond/branch_1_fun/ppermute | solution.py:39
  176.9 6.8 %collective-permute-start.69 = (bf16[128,2048]{1,0:T(8,128)(2,1)}, bf16[128,2048]{1,0:T(8,128)(2,1)S(1)}, u32[]{:S(2)}, u32[]{:S(2)}) collective-permute-start(bf16[128,2048]{1,0:T(8,128)(2,1)} %copy-done.37), channel_id=1, source_target_pairs={{0,2},{1,3},{2,6},{3,7},{4,0},{5,1},{6,4},{7,5},{8,10},{9,11},{10,... | collective-permute-start | bytes 1572872 | tf_op jit(solution)/shard_map/cond/branch_1_fun/ppermute | solution.py:34
  189.3 6.0 %branch_1_fun.36 = bf16[2,384,2048]{2,1,0:T(8,128)(2,1)} custom-call(bf16[128,2048]{1,0:T(8,128)(2,1)S(1)} %collective-permute-done.41.value.refs_0_, bf16[128,2048]{1,0:T(8,128)(2,1)S(1)} %collective-permute-done.71.refs_1_, bf16[128,2048]{1,0:T(8,128)(2,1)S(1)} %copy-done.19, bf16[128,2048]{1,0:T(8,128)(2,1)S(1)} %collective-permute-done.72.refs_3_, ...), custom_call_target="tpu_custom_call" | custom-call | flops 1610612736 | bytes 14434304 | tf_op jit(solution)/shard_map/cond/branch_1_fun/pallas_call | solution.py:94
  197.0 11.1 %collective-permute-done.70.refs_1_ = bf16[128,2048]{1,0:T(8,128)(2,1)S(1)} collective-permute-done((bf16[128,2048]{1,0:T(8,128)(2,1)S(1)}, bf16[128,2048]{1,0:T(8,128)(2,1)S(1)}, u32[]{:S(2)}, u32[]{:S(2)}) %collective-permute-start.70) | collective-permute-done | bytes 524320 | tf_op jit(solution)/shard_map/cond/branch_1_fun/ppermute | solution.py:26
  210.1 14.2 %collective-permute-done.75.refs_2_ = bf16[128,2048]{1,0:T(8,128)(2,1)S(1)} collective-permute-done((bf16[128,2048]{1,0:T(8,128)(2,1)S(1)}, bf16[128,2048]{1,0:T(8,128)(2,1)S(1)}, u32[]{:S(2)}, u32[]{:S(2)}) %collective-permute-start.75) | collective-permute-done | bytes 524320 | tf_op jit(solution)/shard_map/cond/branch_1_fun/ppermute | solution.py:26
  226.0 12.8 %collective-permute-done.77.peer = bf16[2,1024,768]{2,1,0:T(8,128)(2,1)S(1)} collective-permute-done((bf16[2,1024,768]{2,1,0:T(8,128)(2,1)S(1)}, bf16[2,1024,768]{2,1,0:T(8,128)(2,1)S(1)}, u32[]{:S(2)}, u32[]{:S(2)}) %collective-permute-start.77) | collective-permute-done | bytes 3145760 | tf_op jit(solution)/shard_map/cond/branch_1_fun/ppermute | solution.py:39
  238.8 3.6 %branch_1_fun.40.rest_0_ = bf16[2,2048,768]{2,1,0:T(8,128)(2,1)} custom-call(bf16[2,1024,768]{2,1,0:T(8,128)(2,1)S(1)} %get-tuple-element.222.own, bf16[2,1024,768]{2,1,0:T(8,128)(2,1)S(1)} %collective-permute-done.77.peer, bf16[2,2048,768]{2,1,0:T(8,128)(2,1)} %branch_1_fun.34.rest_0_), custom_call_target="tpu_custom_call", output_to_operand_aliasing={{}: (2, {})} | custom-call | bytes 12582912 | tf_op jit(solution)/shard_map/cond/branch_1_fun/pallas_call | solution.py:94
  242.4 10.4 %collective-permute-done.76.peer = bf16[2,256,768]{2,1,0:T(8,128)(2,1)S(1)} collective-permute-done((bf16[2,256,768]{2,1,0:T(8,128)(2,1)}, bf16[2,256,768]{2,1,0:T(8,128)(2,1)S(1)}, u32[]{:S(2)}, u32[]{:S(2)}) %collective-permute-start.76) | collective-permute-done | bytes 786464 | tf_op jit(solution)/shard_map/cond/branch_1_fun/ppermute | solution.py:39
  (140 shorter events, 60.5 us)
Async XLA Ops:
  1.5 30.5 %collective-permute-start.39 = (bf16[128,2048]{1,0:T(8,128)(2,1)}, bf16[128,2048]{1,0:T(8,128)(2,1)S(1)}, u32[]{:S(2)}, u32[]{:S(2)}) collective-permute-start(bf16[128,2048]{1,0:T(8,128)(2,1)} %get-tuple-element.154.value.refs_0_.base), channel_id=1, source_target_pairs={{0,2},{1,3},{2,0},{3,1},{4,6},{5,7},{6,4},{7,5},{8,10},{9,11},{10,... | collective-permute-start | bytes 1572872 | tf_op jit(solution)/shard_map/cond/branch_1_fun/ppermute | solution.py:26
  4.6 27.5 %collective-permute-start.40 = (bf16[128,2048]{1,0:T(8,128)(2,1)}, bf16[128,2048]{1,0:T(8,128)(2,1)S(1)}, u32[]{:S(2)}, u32[]{:S(2)}) collective-permute-start(bf16[128,2048]{1,0:T(8,128)(2,1)} %get-tuple-element.154.value.refs_0_.base), channel_id=1, source_target_pairs={{0,6},{1,7},{2,4},{3,5},{4,2},{5,3},{6,0},{7,1},{8,14},{9,15},{10,... | collective-permute-start | bytes 1572872 | tf_op jit(solution)/shard_map/cond/branch_1_fun/ppermute | solution.py:26
  7.1 13.3 %collective-permute-start.41 = (bf16[128,2048]{1,0:T(8,128)(2,1)}, bf16[128,2048]{1,0:T(8,128)(2,1)S(1)}, u32[]{:S(2)}, u32[]{:S(2)}) collective-permute-start(bf16[128,2048]{1,0:T(8,128)(2,1)} %get-tuple-element.169.value.refs_0_.base), channel_id=1, source_target_pairs={{0,16},{8,24},{16,0},{24,8},{1,17},{9,25},{17,1},{25,9},{2,18},{10... | collective-permute-start | bytes 1572872 | tf_op jit(solution)/shard_map/cond/branch_1_fun/ppermute | solution.py:39
  33.1 13.6 %collective-permute-start.44 = (bf16[2,64,2048]{2,1,0:T(8,128)(2,1)}, bf16[2,64,2048]{2,1,0:T(8,128)(2,1)S(1)}, u32[]{:S(2)}, u32[]{:S(2)}) collective-permute-start(bf16[2,64,2048]{2,1,0:T(8,128)(2,1)} %get-tuple-element.146), channel_id=1, source_target_pairs={{0,16},{8,24},{16,0},{24,8},{1,17},{9,25},{17,1},{25,9},{2,18},{10... | collective-permute-start | bytes 1572872 | tf_op jit(solution)/shard_map/cond/branch_1_fun/ppermute | solution.py:39
  34.7 12.8 %collective-permute-start.43 = (bf16[128,2048]{1,0:T(8,128)(2,1)S(1)}, bf16[128,2048]{1,0:T(8,128)(2,1)S(1)}, u32[]{:S(2)}, u32[]{:S(2)}) collective-permute-start(bf16[128,2048]{1,0:T(8,128)(2,1)S(1)} %branch_1_fun.22), channel_id=1, source_target_pairs={{0,4},{1,5},{2,0},{3,1},{4,6},{5,7},{6,2},{7,3},{8,12},{9,13},{10,... | collective-permute-start | bytes 1572872 | tf_op jit(solution)/shard_map/cond/branch_1_fun/ppermute | solution.py:34
  47.4 29.3 %collective-permute-start.52 = (bf16[2,160,2048]{2,1,0:T(8,128)(2,1)}, bf16[2,160,2048]{2,1,0:T(8,128)(2,1)S(1)}, u32[]{:S(2)}, u32[]{:S(2)}) collective-permute-start(bf16[2,160,2048]{2,1,0:T(8,128)(2,1)} %get-tuple-element.158), channel_id=1, source_target_pairs={{0,16},{8,24},{16,0},{24,8},{1,17},{9,25},{17,1},{25,9},{2,18},{10... | collective-permute-start | bytes 3932168 | tf_op jit(solution)/shard_map/cond/branch_1_fun/ppermute | solution.py:39
  50.4 19.0 %collective-permute-start.46 = (bf16[128,2048]{1,0:T(8,128)(2,1)S(1)}, bf16[128,2048]{1,0:T(8,128)(2,1)S(1)}, u32[]{:S(2)}, u32[]{:S(2)}) collective-permute-start(bf16[128,2048]{1,0:T(8,128)(2,1)S(1)} %copy-done.43), channel_id=1, source_target_pairs={{0,2},{1,3},{2,0},{3,1},{4,6},{5,7},{6,4},{7,5},{8,10},{9,11},{10,... | collective-permute-start | bytes 1572872 | tf_op jit(solution)/shard_map/cond/branch_1_fun/ppermute | solution.py:26
  51.3 25.5 %collective-permute-start.47 = (bf16[128,2048]{1,0:T(8,128)(2,1)S(1)}, bf16[128,2048]{1,0:T(8,128)(2,1)S(1)}, u32[]{:S(2)}, u32[]{:S(2)}) collective-permute-start(bf16[128,2048]{1,0:T(8,128)(2,1)S(1)} %copy-done.43), channel_id=1, source_target_pairs={{0,6},{1,7},{2,4},{3,5},{4,2},{5,3},{6,0},{7,1},{8,14},{9,15},{10,... | collective-permute-start | bytes 1572872 | tf_op jit(solution)/shard_map/cond/branch_1_fun/ppermute | solution.py:26
  77.6 15.5 %collective-permute-start.53 = (bf16[128,2048]{1,0:T(8,128)(2,1)S(1)}, bf16[128,2048]{1,0:T(8,128)(2,1)S(1)}, u32[]{:S(2)}, u32[]{:S(2)}) collective-permute-start(bf16[128,2048]{1,0:T(8,128)(2,1)S(1)} %branch_1_fun.25), channel_id=1, source_target_pairs={{0,4},{1,5},{2,0},{3,1},{4,6},{5,7},{6,2},{7,3},{8,12},{9,13},{10,... | collective-permute-start | bytes 1572872 | tf_op jit(solution)/shard_map/cond/branch_1_fun/ppermute | solution.py:34
  79.5 13.6 %collective-permute-start.55 = (bf16[2,64,2048]{2,1,0:T(8,128)(2,1)S(1)}, bf16[2,64,2048]{2,1,0:T(8,128)(2,1)S(1)}, u32[]{:S(2)}, u32[]{:S(2)}) collective-permute-start(bf16[2,64,2048]{2,1,0:T(8,128)(2,1)S(1)} %copy-done.51), channel_id=1, source_target_pairs={{0,16},{8,24},{16,0},{24,8},{1,17},{9,25},{17,1},{25,9},{2,18},{10... | collective-permute-start | bytes 1572872 | tf_op jit(solution)/shard_map/cond/branch_1_fun/ppermute | solution.py:39
  93.1 24.0 %collective-permute-start.62 = (bf16[2,512,512]{2,1,0:T(8,128)(2,1)S(1)}, bf16[2,512,512]{2,1,0:T(8,128)(2,1)S(1)}, u32[]{:S(2)}, u32[]{:S(2)}) collective-permute-start(bf16[2,512,512]{2,1,0:T(8,128)(2,1)S(1)} %get-tuple-element.183.refs_9_), channel_id=1, source_target_pairs={{0,16},{8,24},{16,0},{24,8},{1,17},{9,25},{17,1},{25,9},{2,18},{10... | collective-permute-start | bytes 3145736 | tf_op jit(solution)/shard_map/cond/branch_1_fun/ppermute | solution.py:39
  94.3 48.0 %collective-permute-start.59 = (bf16[128,2048]{1,0:T(8,128)(2,1)S(1)}, bf16[128,2048]{1,0:T(8,128)(2,1)S(1)}, u32[]{:S(2)}, u32[]{:S(2)}) collective-permute-start(bf16[128,2048]{1,0:T(8,128)(2,1)S(1)} %collective-permute-done.41.value.refs_0_), channel_id=1, source_target_pairs={{0,2},{1,3},{2,0},{3,1},{4,6},{5,7},{6,4},{7,5},{8,10},{9,11},{10,... | collective-permute-start | bytes 1572872 | tf_op jit(solution)/shard_map/cond/branch_1_fun/ppermute | solution.py:26
  94.5 47.8 %collective-permute-start.60 = (bf16[128,2048]{1,0:T(8,128)(2,1)S(1)}, bf16[128,2048]{1,0:T(8,128)(2,1)S(1)}, u32[]{:S(2)}, u32[]{:S(2)}) collective-permute-start(bf16[128,2048]{1,0:T(8,128)(2,1)S(1)} %collective-permute-done.41.value.refs_0_), channel_id=1, source_target_pairs={{0,6},{1,7},{2,4},{3,5},{4,2},{5,3},{6,0},{7,1},{8,14},{9,15},{10,... | collective-permute-start | bytes 1572872 | tf_op jit(solution)/shard_map/cond/branch_1_fun/ppermute | solution.py:26
  96.9 39.4 %collective-permute-start.63 = (bf16[128,2048]{1,0:T(8,128)(2,1)S(1)}, bf16[128,2048]{1,0:T(8,128)(2,1)S(1)}, u32[]{:S(2)}, u32[]{:S(2)}) collective-permute-start(bf16[128,2048]{1,0:T(8,128)(2,1)S(1)} %get-tuple-element.192), channel_id=1, source_target_pairs={{0,2},{1,3},{2,6},{3,7},{4,0},{5,1},{6,4},{7,5},{8,10},{9,11},{10,... | collective-permute-start | bytes 1572872 | tf_op jit(solution)/shard_map/cond/branch_1_fun/ppermute | solution.py:34
  96.9 45.4 %collective-permute-start.64 = (bf16[128,2048]{1,0:T(8,128)(2,1)S(1)}, bf16[128,2048]{1,0:T(8,128)(2,1)S(1)}, u32[]{:S(2)}, u32[]{:S(2)}) collective-permute-start(bf16[128,2048]{1,0:T(8,128)(2,1)S(1)} %get-tuple-element.193), channel_id=1, source_target_pairs={{0,2},{1,3},{2,0},{3,1},{4,6},{5,7},{6,4},{7,5},{8,10},{9,11},{10,... | collective-permute-start | bytes 1572872 | tf_op jit(solution)/shard_map/cond/branch_1_fun/ppermute | solution.py:26
  117.2 54.2 %collective-permute-start.67 = (bf16[2,768,768]{2,1,0:T(8,128)(2,1)S(1)}, bf16[2,768,768]{2,1,0:T(8,128)(2,1)S(1)}, u32[]{:S(2)}, u32[]{:S(2)}) collective-permute-start(bf16[2,768,768]{2,1,0:T(8,128)(2,1)S(1)} %get-tuple-element.202.own), channel_id=1, source_target_pairs={{0,16},{8,24},{16,0},{24,8},{1,17},{9,25},{17,1},{25,9},{2,18},{10... | collective-permute-start | bytes 7077896 | tf_op jit(solution)/shard_map/cond/branch_1_fun/ppermute | solution.py:39
  143.1 95.7 %collective-permute-start.77 = (bf16[2,1024,768]{2,1,0:T(8,128)(2,1)S(1)}, bf16[2,1024,768]{2,1,0:T(8,128)(2,1)S(1)}, u32[]{:S(2)}, u32[]{:S(2)}) collective-permute-start(bf16[2,1024,768]{2,1,0:T(8,128)(2,1)S(1)} %get-tuple-element.222.own), channel_id=1, source_target_pairs={{0,16},{8,24},{16,0},{24,8},{1,17},{9,25},{17,1},{25,9},{2,18},{10... | collective-permute-start | bytes 9437192 | tf_op jit(solution)/shard_map/cond/branch_1_fun/ppermute | solution.py:39
  144.4 29.7 %collective-permute-start.68 = (bf16[128,2048]{1,0:T(8,128)(2,1)S(1)}, bf16[128,2048]{1,0:T(8,128)(2,1)S(1)}, u32[]{:S(2)}, u32[]{:S(2)}) collective-permute-start(bf16[128,2048]{1,0:T(8,128)(2,1)S(1)} %branch_1_fun.35), channel_id=1, source_target_pairs={{0,6},{1,7},{2,4},{3,5},{4,2},{5,3},{6,0},{7,1},{8,14},{9,15},{10,... | collective-permute-start | bytes 1572872 | tf_op jit(solution)/shard_map/cond/branch_1_fun/ppermute | solution.py:26
  145.3 29.6 %collective-permute-start.66 = (bf16[128,2048]{1,0:T(8,128)(2,1)S(1)}, bf16[128,2048]{1,0:T(8,128)(2,1)S(1)}, u32[]{:S(2)}, u32[]{:S(2)}) collective-permute-start(bf16[128,2048]{1,0:T(8,128)(2,1)S(1)} %branch_1_fun.32), channel_id=1, source_target_pairs={{0,4},{1,5},{2,0},{3,1},{4,6},{5,7},{6,2},{7,3},{8,12},{9,13},{10,... | collective-permute-start | bytes 1572872 | tf_op jit(solution)/shard_map/cond/branch_1_fun/ppermute | solution.py:34
  175.6 12.6 %collective-permute-start.74 = (bf16[128,2048]{1,0:T(8,128)(2,1)S(1)}, bf16[128,2048]{1,0:T(8,128)(2,1)S(1)}, u32[]{:S(2)}, u32[]{:S(2)}) collective-permute-start(bf16[128,2048]{1,0:T(8,128)(2,1)S(1)} %collective-permute-done.60.far.refs_6_), channel_id=1, source_target_pairs={{0,1},{1,0},{2,3},{3,2},{4,5},{5,4},{6,7},{7,6},{8,9},{9,8},{10,11... | collective-permute-start | bytes 1572872 | tf_op jit(solution)/shard_map/cond/branch_1_fun/ppermute | solution.py:26
  176.9 20.1 %collective-permute-start.69 = (bf16[128,2048]{1,0:T(8,128)(2,1)}, bf16[128,2048]{1,0:T(8,128)(2,1)S(1)}, u32[]{:S(2)}, u32[]{:S(2)}) collective-permute-start(bf16[128,2048]{1,0:T(8,128)(2,1)} %copy-done.37), channel_id=1, source_target_pairs={{0,2},{1,3},{2,6},{3,7},{4,0},{5,1},{6,4},{7,5},{8,10},{9,11},{10,... | collective-permute-start | bytes 1572872 | tf_op jit(solution)/shard_map/cond/branch_1_fun/ppermute | solution.py:34
  183.6 24.5 %collective-permute-start.70 = (bf16[128,2048]{1,0:T(8,128)(2,1)S(1)}, bf16[128,2048]{1,0:T(8,128)(2,1)S(1)}, u32[]{:S(2)}, u32[]{:S(2)}) collective-permute-start(bf16[128,2048]{1,0:T(8,128)(2,1)S(1)} %copy-done.35), channel_id=1, source_target_pairs={{0,2},{1,3},{2,0},{3,1},{4,6},{5,7},{6,4},{7,5},{8,10},{9,11},{10,... | collective-permute-start | bytes 1572872 | tf_op jit(solution)/shard_map/cond/branch_1_fun/ppermute | solution.py:26
  184.4 68.4 %collective-permute-start.76 = (bf16[2,256,768]{2,1,0:T(8,128)(2,1)}, bf16[2,256,768]{2,1,0:T(8,128)(2,1)S(1)}, u32[]{:S(2)}, u32[]{:S(2)}) collective-permute-start(bf16[2,256,768]{2,1,0:T(8,128)(2,1)} %get-tuple-element.186.own), channel_id=1, source_target_pairs={{0,16},{8,24},{16,0},{24,8},{1,17},{9,25},{17,1},{25,9},{2,18},{10... | collective-permute-start | bytes 2359304 | tf_op jit(solution)/shard_map/cond/branch_1_fun/ppermute | solution.py:39
  208.5 15.8 %collective-permute-start.75 = (bf16[128,2048]{1,0:T(8,128)(2,1)S(1)}, bf16[128,2048]{1,0:T(8,128)(2,1)S(1)}, u32[]{:S(2)}, u32[]{:S(2)}) collective-permute-start(bf16[128,2048]{1,0:T(8,128)(2,1)S(1)} %branch_1_fun.38), channel_id=1, source_target_pairs={{0,6},{1,7},{2,4},{3,5},{4,2},{5,3},{6,0},{7,1},{8,14},{9,15},{10,... | collective-permute-start | bytes 1572872 | tf_op jit(solution)/shard_map/cond/branch_1_fun/ppermute | solution.py:26
  (42 other events, 410.8 us)
